TPU v7x, 32 devices: a whole 2x2x4 slice. The times are simulated.
32 devices in a mesh: grp: 2 (over y), hor: 8 (over z, x), blk: 2 (over core).
Axes of the slice: x: 2, y: 2, z: 4, core: 2. Of those that a mesh axis runs over, the one named last changes fastest.
Arguments:
- hessian_part: float32 [16, 1024, 512], P(('grp', 'hor'), 'blk'), parts along dimension 0, as said below
- coupling: float32 [16, 512, 512], P(('grp', 'hor'), None, 'blk'), parts along dimension 0, may hold values from -1 to 1, as said below
- rhs: float32 [16, 512, 256], P(('grp', 'hor'), None, 'blk'), parts along dimension 0, may hold values from -6 to 6
Outputs:
- reduced_diag: float32 [16, 512, 512], P(('grp', 'hor'), None, 'blk'), parts along dimension 0
- reduced_coupling: float32 [16, 512, 512], P(('grp', 'hor'), None, 'blk'), parts along dimension 0
- reduced_rhs: float32 [16, 512, 256], P(('grp', 'hor'), None, 'blk'), parts along dimension 0
There are 2 independent parts, one for each index of `grp`. A program takes and returns all parts, laid end to end along the dimension named above; each array names one. Nothing has to cross between parts.
Inputs may be any that keep to these rules, and one draw needn't show every extreme that they name: `hessian_part`: each partial block is symmetric positive definite. `coupling`: together with the summed Hessian blocks, the block tridiagonal matrix of all 8 sections is symmetric positive definite.
All inputs are finite; a program needn't handle non-finite values.
Results may differ from a plain program's by a relative error of at most 0.0003.
Values sent between devices are 32-bit elements; how exact they have to be, the bound alone decides.
A program may use at most 64 MiB of HBM per device.

v0:
```python
import jax
import jax.numpy as jnp
from jax import lax
from jax.sharding import PartitionSpec as P

LEVELS = 2


def shifted(block, axis, distance):
    devices = range(lax.axis_size(axis))
    route = [(i - distance, i) for i in devices if i - distance in devices]
    return lax.ppermute(block, axis, route)


def product_of(left, right):
    return jnp.dot(left, right, precision=lax.Precision.HIGHEST, preferred_element_type=jnp.float32)


def shards(hessian_part, coupling, rhs):
    order_full = coupling.shape[1]
    half_width = coupling.shape[2]
    blk_index = lax.axis_index("blk")
    section_index = lax.axis_index("hor")
    partial_value = hessian_part[0]
    link_half = coupling[0]
    link_half = jnp.where(section_index >= 1, link_half, jnp.zeros_like(link_half))
    right_half = rhs[0]
    diag_full = lax.psum(partial_value, "blk")
    diag_half = lax.dynamic_slice_in_dim(diag_full, blk_index * half_width, half_width, 1)
    link_full = lax.all_gather(link_half, "blk", axis=1, tiled=True)
    identity = jnp.eye(order_full, dtype=jnp.float32)
    for depth in range(LEVELS):
        if depth > 0:
            diag_full, link_full = (
                lax.all_gather(diag_half, "blk", axis=1, tiled=True),
                lax.all_gather(link_half, "blk", axis=1, tiled=True),
            )
        distance = 2**depth
        factor = jnp.linalg.cholesky(diag_full)
        inverse = lax.linalg.triangular_solve(factor, identity, left_side=True, lower=True)
        scaled = product_of(inverse, right_half)
        product = product_of(inverse, link_full)
        upward = jnp.concatenate([inverse, product, scaled], 1)
        downward = jnp.concatenate([product, scaled], 1)
        from_lower = shifted(upward, "hor", distance)
        from_upper = shifted(downward, "hor", -distance)
        inverse_low = from_lower[:, :order_full]
        product_low = from_lower[:, order_full : 2 * order_full]
        scaled_low = from_lower[:, 2 * order_full :]
        product_high = from_upper[:, :order_full]
        scaled_high = from_upper[:, order_full:]
        left_gram = product_of(link_full, inverse_low.T)
        gram_rows = lax.dynamic_slice_in_dim(left_gram, blk_index * half_width, half_width, 0)
        low_cols = lax.dynamic_slice_in_dim(product_low, blk_index * half_width, half_width, 1)
        high_cols = lax.dynamic_slice_in_dim(product_high, blk_index * half_width, half_width, 1)
        new_diag = (
            diag_half - product_of(left_gram, gram_rows.T) - product_of(product_high.T, high_cols)
        )
        new_link = -product_of(left_gram, low_cols)
        new_right = (
            right_half - product_of(left_gram, scaled_low) - product_of(product_high.T, scaled_high)
        )
        diag_half, link_half, right_half = (new_diag, new_link, new_right)
    return (diag_half[None], link_half[None], right_half[None])


def solution(mesh):
    return jax.shard_map(
        shards,
        mesh=mesh,
        in_specs=(
            P(("grp", "hor"), "blk", None),
            P(("grp", "hor"), None, "blk"),
            P(("grp", "hor"), None, "blk"),
        ),
        out_specs=(
            P(("grp", "hor"), None, "blk"),
            P(("grp", "hor"), None, "blk"),
            P(("grp", "hor"), None, "blk"),
        ),
        check_vma=False,
    )
```

profile of v0, /device:TPU:0, one launch (start us, length us, event | category | flops | bytes accessed | tf_op | source)
XLA Modules:
  0.0 522.2 jit_solution(15809350621695954749)
XLA Ops:
  7.2 2.6 copy.6
  11.0 21.7 %all-reduce.3.cloned.1.call-done = f32[512,512]{0,1:T(8,128)} async-done(((f32[512,512]{0,1:T(8,128)}), f32[512,512]{0,1:T(8,128)}) %all-reduce.3.cloned.1.call-update) | async-done | bytes 1048592 | tf_op jit(solution)/shard_map/psum | solution.py:28
  35.5 11.7 %cholesky.286 = f32[128,128]{1,0:T(8,128)S(1)} custom-call(f32[128,128]{1,0:T(8,128)S(1)} %cholesky.426), custom_call_target="Cholesky" | custom-call | tf_op jit(solution)/shard_map/jit(cholesky)/cholesky | solution.py:39
  47.4 9.8 %custom-call.27 = f32[1,128,128]{1,2,0:T(8,128)S(1)} custom-call(f32[1,128,128]{2,1,0:T(8,128)S(1)} %get-tuple-element.63), custom_call_target="InvertDiagBlocksLowerTriangular" | custom-call | tf_op jit(solution)/shard_map/jit(cholesky)/cholesky | solution.py:39
  59.8 11.7 %cholesky.305 = f32[128,128]{1,0:T(8,128)S(1)} custom-call(f32[128,128]{1,0:T(8,128)S(1)} %cholesky.430), custom_call_target="Cholesky" | custom-call | tf_op jit(solution)/shard_map/jit(cholesky)/cholesky | solution.py:39
  71.5 10.0 %custom-call.28 = f32[1,128,128]{1,2,0:T(8,128)S(1)} custom-call(f32[1,128,128]{2,1,0:T(8,128)S(1)} %get-tuple-element.60), custom_call_target="InvertDiagBlocksLowerTriangular" | custom-call | tf_op jit(solution)/shard_map/jit(cholesky)/cholesky | solution.py:39
  83.1 11.7 %cholesky.326 = f32[128,128]{1,0:T(8,128)S(1)} custom-call(f32[128,128]{1,0:T(8,128)S(1)} %cholesky.435), custom_call_target="Cholesky" | custom-call | tf_op jit(solution)/shard_map/jit(cholesky)/cholesky | solution.py:39
  94.9 9.8 %custom-call.29 = f32[1,128,128]{1,2,0:T(8,128)S(1)} custom-call(f32[1,128,128]{2,1,0:T(8,128)S(1)} %get-tuple-element.57), custom_call_target="InvertDiagBlocksLowerTriangular" | custom-call | tf_op jit(solution)/shard_map/jit(cholesky)/cholesky | solution.py:39
  106.1 11.7 %cholesky.343 = f32[128,128]{1,0:T(8,128)S(1)} custom-call(f32[128,128]{1,0:T(8,128)S(1)} %convolution_subtract_fusion.17), custom_call_target="Cholesky" | custom-call | tf_op jit(solution)/shard_map/jit(cholesky)/cholesky | solution.py:39
  132.6 12.0 %while.4 = (s32[]{:T(128)}, f32[512,512]{1,0:T(8,128)}, s32[4,2]{0,1:T(2,128)S(1)}, f32[4,128,128]{2,1,0:T(8,128)S(1)}, s32[]{:T(128)}) while((s32[]{:T(128)}, f32[512,512]{1,0:T(8,128)}, s32[4,2]{0,1:T(2,128)S(1)}, f32[4,128,128]{2,1,0:T(8,128)S(1)}, s32[]{:T(128)}) %tuple.56), condition=%wide.while_cond, body=%wide.while_body.sunk | while | flops 2 | bytes 131189 | solution.py:40
  136.3 2.3 bitcast_dynamic-update-slice_fusion.4
  144.6 39.3 %custom-call.30 = f32[4,128,128]{1,2,0:T(8,128)S(1)} custom-call(f32[4,128,128]{2,1,0:T(8,128)S(1)} %get-tuple-element.19), custom_call_target="InvertDiagBlocksLowerTriangular" | custom-call | tf_op jit(solution)/shard_map/triangular_solve/custom-call.3 | solution.py:40
  192.7 3.3 fusion.12
  197.4 3.1 pad_maximum_fusion
  200.6 5.1 collective-permute-start
  208.2 31.5 %collective-permute-done.1 = f32[512,640]{0,1:T(8,128)S(1)} collective-permute-done((f32[512,640]{0,1:T(8,128)}, f32[512,640]{0,1:T(8,128)S(1)}, u32[]{:S(2)}, u32[]{:S(2)}) %collective-permute-start.1) | collective-permute-done | bytes 1310752 | tf_op jit(solution)/shard_map/ppermute | solution.py:12
  240.8 42.8 %collective-permute-done = f32[512,1152]{1,0:T(8,128)} collective-permute-done((f32[512,1152]{1,0:T(8,128)}, f32[512,1152]{1,0:T(8,128)}, u32[]{:S(2)}, u32[]{:S(2)}) %collective-permute-start) | collective-permute-done | bytes 2359328 | tf_op jit(solution)/shard_map/ppermute | solution.py:12
  283.5 3.2 fusion.7
  297.6 4.3 all-gather.7.cloned.1.call-done
  304.7 11.7 %cholesky.358 = f32[128,128]{1,0:T(8,128)S(1)} custom-call(f32[128,128]{1,0:T(8,128)S(1)} %cholesky.439), custom_call_target="Cholesky" | custom-call | tf_op jit(solution)/shard_map/jit(cholesky)/cholesky | solution.py:39
  316.6 9.8 %custom-call.31 = f32[1,128,128]{1,2,0:T(8,128)S(1)} custom-call(f32[1,128,128]{2,1,0:T(8,128)S(1)} %get-tuple-element.53), custom_call_target="InvertDiagBlocksLowerTriangular" | custom-call | tf_op jit(solution)/shard_map/jit(cholesky)/cholesky | solution.py:39
  328.9 11.9 %cholesky.377 = f32[128,128]{1,0:T(8,128)S(1)} custom-call(f32[128,128]{1,0:T(8,128)S(1)} %cholesky.443), custom_call_target="Cholesky" | custom-call | tf_op jit(solution)/shard_map/jit(cholesky)/cholesky | solution.py:39
  340.9 9.8 %custom-call.32 = f32[1,128,128]{1,2,0:T(8,128)S(1)} custom-call(f32[1,128,128]{2,1,0:T(8,128)S(1)} %get-tuple-element.50), custom_call_target="InvertDiagBlocksLowerTriangular" | custom-call | tf_op jit(solution)/shard_map/jit(cholesky)/cholesky | solution.py:39
  352.2 11.7 %cholesky.398 = f32[128,128]{1,0:T(8,128)S(1)} custom-call(f32[128,128]{1,0:T(8,128)S(1)} %cholesky.448), custom_call_target="Cholesky" | custom-call | tf_op jit(solution)/shard_map/jit(cholesky)/cholesky | solution.py:39
  364.0 9.8 %custom-call.33 = f32[1,128,128]{1,2,0:T(8,128)S(1)} custom-call(f32[1,128,128]{2,1,0:T(8,128)S(1)} %get-tuple-element.47), custom_call_target="InvertDiagBlocksLowerTriangular" | custom-call | tf_op jit(solution)/shard_map/jit(cholesky)/cholesky | solution.py:39
  375.2 11.9 %cholesky.415 = f32[128,128]{1,0:T(8,128)S(1)} custom-call(f32[128,128]{1,0:T(8,128)S(1)} %convolution_subtract_fusion.16), custom_call_target="Cholesky" | custom-call | tf_op jit(solution)/shard_map/jit(cholesky)/cholesky | solution.py:39
  392.5 7.9 %while.5 = (s32[]{:T(128)}, f32[512,512]{1,0:T(8,128)S(1)}, s32[4,2]{0,1:T(2,128)S(1)}, f32[4,128,128]{2,1,0:T(8,128)S(1)}, s32[]{:T(128)}) while((s32[]{:T(128)}, f32[512,512]{1,0:T(8,128)S(1)}, s32[4,2]{0,1:T(2,128)S(1)}, f32[4,128,128]{2,1,0:T(8,128)S(1)}, s32[]{:T(128)}) %tuple.70), condition=%wide.while_cond.clone, body=%wide.while_body.clone.sunk | while | flops 2 | bytes 131189 | solution.py:40
  400.4 39.3 %custom-call.34 = f32[4,128,128]{1,2,0:T(8,128)S(1)} custom-call(f32[4,128,128]{2,1,0:T(8,128)S(1)} %get-tuple-element.20), custom_call_target="InvertDiagBlocksLowerTriangular" | custom-call | tf_op jit(solution)/shard_map/triangular_solve/custom-call.3 | solution.py:40
  446.5 3.1 fusion.26
  450.2 3.8 collective-permute-start.2
  455.8 31.0 %collective-permute-done.3 = f32[512,640]{0,1:T(8,128)S(1)} collective-permute-done((f32[512,640]{0,1:T(8,128)S(1)}, f32[512,640]{0,1:T(8,128)S(1)}, u32[]{:S(2)}, u32[]{:S(2)}) %collective-permute-start.3) | collective-permute-done | bytes 1310752 | tf_op jit(solution)/shard_map/ppermute | solution.py:12
  488.6 16.2 %collective-permute-done.2 = f32[512,1152]{1,0:T(8,128)S(1)} collective-permute-done((f32[512,1152]{1,0:T(8,128)S(1)}, f32[512,1152]{1,0:T(8,128)S(1)}, u32[]{:S(2)}, u32[]{:S(2)}) %collective-permute-start.2) | collective-permute-done | bytes 2359328 | tf_op jit(solution)/shard_map/ppermute | solution.py:12
  (166 shorter events, 87.2 us)
Async XLA Ops:
  7.2 2.8 copy-start.18
  7.2 25.5 %all-reduce.3.cloned.1.call-start = ((), (), s32[]{:S(2)}) async-start(), calls=%async_computation | async-start | bytes 2097152 | tf_op jit(solution)/shard_map/psum | solution.py:28
  9.9 182.9 %all-gather.9.cloned.1.call-start = ((), (), s32[]{:S(2)}) async-start(), calls=%async_computation.3 | async-start | bytes 1572864 | tf_op jit(solution)/shard_map/all_gather | solution.py:30
  10.8 291.1 %all-gather.7.cloned.1.call-start = ((), (), s32[]{:S(2)}) async-start(), calls=%async_computation.2 | async-start | bytes 1572864 | tf_op jit(solution)/shard_map/all_gather | solution.py:35
  32.7 1.7 copy-start
  34.6 1.0 copy-start.9
  185.5 5.1 copy-start.20
  186.0 4.0 copy-start.1
  187.8 2.1 copy-start.7
  189.9 0.7 copy-start.10
  191.9 0.8 copy-start.11
  197.4 8.2 %copy-start.12 = (f32[512,128]{0,1:T(8,128)S(1)}, f32[512,128]{0,1:T(8,128)}, u32[]{:S(2)}) copy-start(f32[512,128]{0,1:T(8,128)} %copy-done.11) | copy-start | bytes 786436
  200.6 83.0 %collective-permute-start = (f32[512,1152]{1,0:T(8,128)}, f32[512,1152]{1,0:T(8,128)}, u32[]{:S(2)}, u32[]{:S(2)}) collective-permute-start(f32[512,1152]{1,0:T(8,128)} %pad_maximum_fusion), channel_id=1, source_target_pairs={{0,2},{2,4},{4,6},{6,8},{8,10},{10,12},{12,14},{1,3},{3,5},{5,7},{... | collective-permute-start | bytes 7077896 | tf_op jit(solution)/shard_map/ppermute | solution.py:12
  206.9 32.8 %collective-permute-start.1 = (f32[512,640]{0,1:T(8,128)}, f32[512,640]{0,1:T(8,128)S(1)}, u32[]{:S(2)}, u32[]{:S(2)}) collective-permute-start(f32[512,640]{0,1:T(8,128)} %pad_maximum_fusion.2), channel_id=1, source_target_pairs={{2,0},{4,2},{6,4},{8,6},{10,8},{12,10},{14,12},{3,1},{5,3},{7,5},{... | collective-permute-start | bytes 3932168 | tf_op jit(solution)/shard_map/ppermute | solution.py:12
  208.2 75.4 %copy-start.4 = (f32[1,512,512]{2,1,0:T(8,128)S(1)}, f32[1,512,512]{2,1,0:T(8,128)}, u32[]{:S(2)}) copy-start(f32[1,512,512]{2,1,0:T(8,128)} %all-gather.9.cloned.1.call-done) | copy-start | bytes 3145732
  239.6 1.1 copy-start.3
  283.5 4.3 slice-start
  289.7 156.8 %all-gather.5.cloned.1.call-start = ((), (), s32[]{:S(2)}) async-start(), calls=%async_computation.1 | async-start | bytes 1572864 | tf_op jit(solution)/shard_map/all_gather | solution.py:36
  292.4 3.2 copy-start.21
  297.5 147.1 %copy-start.16 = (f32[512,128]{1,0:T(8,128)}, f32[512,128]{1,0:T(8,128)S(1)}, u32[]{:S(2)}) copy-start(f32[512,128]{1,0:T(8,128)S(1)} %fusion.4) | copy-start | bytes 786436
  301.9 1.7 copy-start.6
  303.7 1.0 copy-start.8
  439.7 0.8 copy-start.19
  445.8 0.7 copy-start.13
  450.0 4.0 copy-start.14
  450.2 54.6 %collective-permute-start.2 = (f32[512,1152]{1,0:T(8,128)S(1)}, f32[512,1152]{1,0:T(8,128)S(1)}, u32[]{:S(2)}, u32[]{:S(2)}) collective-permute-start(f32[512,1152]{1,0:T(8,128)S(1)} %pad_maximum_fusion.1), channel_id=1, source_target_pairs={{0,4},{2,6},{4,8},{6,10},{8,12},{10,14},{1,5},{3,7},{5,9},{7,11},{... | collective-permute-start | bytes 7077896 | tf_op jit(solution)/shard_map/ppermute | solution.py:12
  454.1 50.7 %copy-start.5 = (f32[512,512]{1,0:T(8,128)S(1)}, f32[512,512]{1,0:T(8,128)}, u32[]{:S(2)}) copy-start(f32[512,512]{1,0:T(8,128)} %all-gather.5.cloned.1.call-done) | copy-start | bytes 3145732
  454.1 32.7 %collective-permute-start.3 = (f32[512,640]{0,1:T(8,128)S(1)}, f32[512,640]{0,1:T(8,128)S(1)}, u32[]{:S(2)}, u32[]{:S(2)}) collective-permute-start(f32[512,640]{0,1:T(8,128)S(1)} %pad_maximum_fusion.3), channel_id=1, source_target_pairs={{4,0},{6,2},{8,4},{10,6},{12,8},{14,10},{5,1},{7,3},{9,5},{11,7},{... | collective-permute-start | bytes 3932168 | tf_op jit(solution)/shard_map/ppermute | solution.py:12
  486.9 19.7 %copy-start.2 = (f32[512,256]{0,1:T(8,128)S(1)}, f32[512,256]{0,1:T(8,128)}, u32[]{:S(2)}) copy-start(f32[512,256]{0,1:T(8,128)} %convolution_subtract_fusion.2) | copy-start | bytes 1572868
  511.6 1.9 copy-start.15
  511.6 1.9 copy-start.17
Sparse Core Ops, SparseCore 0:
  10.3 22.2 all-reduce.2
  34.9 10.3 all-gather.8
  289.8 11.9 all-gather.6
  303.9 10.2 all-gather.4
where the time goes:
time: 532 us; the launch traced here: 522 us
  other arithmetic  244 us (46%)
  waiting for transfers between devices  148 us (28%)
  matrix products  52.6 us (10%)
  local copies, waits for them, and re-layouts  36.5 us (7%)
  between operations  29.1 us (5%)
  starting transfers between devices  12.4 us (2%)
    another operation x29, other arithmetic, shards(): factor = jnp.linalg.cholesky(diag_full)  158 us
    ppermute x4, waiting for transfers between devices, shifted(): return lax.ppermute(block, axis, route)  121 us
    another operation x5, other arithmetic, shards(): lax.linalg.triangular_solve(factor, identity, left_side=True, lower=True)  79.9 us
    dot_general x16, matrix products, product_of(): jnp.dot(left, right, precision=lax.Precision.HIGHEST, preferred_element_t...  30.9 us
    psum x1, waiting for transfers between devices, shards(): diag_full = lax.psum(partial_value, 'blk')  21.7 us
    another operation x27, local copies, waits for them, and re-layouts, shards(): lax.linalg.triangular_solve(factor, identity, left_side=True, lower=True)  19.7 us
    ppermute x4, starting transfers between devices, shifted(): return lax.ppermute(block, axis, route)  11.8 us
    another operation x12, matrix products, shards(): factor = jnp.linalg.cholesky(diag_full)  10.9 us
  transfers between devices with their start and end apart: 8, of which 6 were waited for; matrix products, arithmetic and copies ran while one was open for 57% of the time, Pallas kernels for 0%

commit v1 on v0

v1 whole, which is shorter than its diff:
```python
import functools

import jax
import jax.numpy as jnp
from jax import lax
from jax.experimental import pallas as pl
from jax.experimental.pallas import tpu as pltpu
from jax.sharding import PartitionSpec as P

LEVELS = 2
ROWS = 8
BASE = 128
NN = (((1,), (0,)), ((), ()))
NT = (((1,), (1,)), ((), ()))
TN = (((0,), (0,)), ((), ()))


def split(x):
    high = x.astype(jnp.bfloat16)
    return high, (x - high.astype(jnp.float32)).astype(jnp.bfloat16)


def multiply(a, b, dims=NN):
    dot = functools.partial(lax.dot_general, dimension_numbers=dims, preferred_element_type=jnp.float32)
    return dot(a[0], b[0]) + (dot(a[0], b[1]) + dot(a[1], b[0]))


def sweep_base(tiles):
    width = tiles[0].shape[1]
    shape = (ROWS, width)
    lane = lax.broadcasted_iota(jnp.int32, shape, 1)
    sub = lax.broadcasted_iota(jnp.int32, shape, 0)
    count = len(tiles)
    for p in range(count):
        first = p * ROWS
        block = tiles[p]
        columns = [
            [jnp.broadcast_to(tiles[q][:, first + l : first + l + 1], shape) for l in range(ROWS)] for q in range(count)
        ]
        e = {
            (i, j): jnp.broadcast_to(columns[p][j][i : i + 1, :], shape) for i in range(ROWS) for j in range(i + 1)
        }
        at = lambda i, j: (max(i, j), min(i, j))
        for k in range(ROWS):
            inv = 1.0 / e[k, k]
            others = [i for i in range(ROWS) if i != k]
            col = {i: e[at(i, k)] for i in others}
            scaled = {i: col[i] * inv for i in others}
            for i in others:
                for j in others:
                    if j <= i:
                        e[i, j] = e[i, j] - scaled[i] * col[j]
            for i in others:
                e[at(i, k)] = scaled[i]
            e[k, k] = -inv
        negated = []
        for l in range(ROWS):
            value = e[at(0, l)]
            for i in range(1, ROWS):
                value = jnp.where(sub == i, e[at(i, l)], value)
            negated.append(value)
        rows = None
        for l in range(ROWS):
            term = negated[l] * jnp.broadcast_to(block[l : l + 1, :], shape)
            rows = -term if rows is None else rows - term
        for l in range(ROWS):
            rows = jnp.where(lane == first + l, negated[l], rows)
        spread = [jnp.broadcast_to(rows[l : l + 1, :], shape) for l in range(ROWS)]
        inside = (lane >= first) & (lane < first + ROWS)
        for q in range(count):
            if q == p:
                continue
            value = jnp.where(inside, 0.0, tiles[q])
            for l in range(ROWS):
                value = value - columns[q][l] * spread[l]
            tiles[q] = value
        tiles[p] = rows
    return tiles


def sweep_all(work, base):
    order = work.shape[0]

    def step(k, carry):
        start = pl.multiple_of(k * BASE, BASE)
        tiles = [work[pl.ds(pl.multiple_of(start + r * ROWS, ROWS), ROWS), pl.ds(start, BASE)] for r in range(BASE // ROWS)]
        for r, tile in enumerate(sweep_base(tiles)):
            base[pl.ds(r * ROWS, ROWS), :] = tile
        negated = base[...]
        panel = split(work[:, pl.ds(start, BASE)])
        rows = -multiply(split(negated), split(work[pl.ds(start, BASE), :]))
        work[pl.ds(start, BASE), :] = rows
        work[pl.ds(start, BASE), pl.ds(start, BASE)] = negated
        rows = work[pl.ds(start, BASE), :]
        work[:, pl.ds(start, BASE)] = jnp.zeros((order, BASE), jnp.float32)
        work[...] = work[...] - multiply(panel, split(rows))
        work[pl.ds(start, BASE), :] = rows
        return carry

    lax.fori_loop(0, order // BASE, step, 0)


def invert_pair_kernel(a_ref, b_ref, total_ref, out_ref, work, base):
    total_ref[...] = a_ref[...] + b_ref[...]
    work[...] = total_ref[...]
    sweep_all(work, base)
    out_ref[...] = work[...]


def invert_kernel(a_ref, out_ref, work, base):
    work[...] = a_ref[...]
    sweep_all(work, base)
    out_ref[...] = work[...]


VMEM = pl.BlockSpec(memory_space=pltpu.VMEM)


def local_call(kernel, ins, outs, scratch, flops, name):
    return pl.pallas_call(
        kernel,
        out_shape=[jax.ShapeDtypeStruct(s, jnp.float32) for s in outs],
        in_specs=[VMEM] * len(ins),
        out_specs=[VMEM] * len(outs),
        scratch_shapes=scratch,
        compiler_params=pltpu.CompilerParams(vmem_limit_bytes=48 * 2**20),
        cost_estimate=pl.CostEstimate(flops=flops, bytes_accessed=4 * 2**20, transcendentals=0),
        name=name,
    )(*ins)


def invert(ins, order):
    scratch = [pltpu.VMEM((order, order), jnp.float32), pltpu.VMEM((BASE, BASE), jnp.float32)]
    square = (order, order)
    if len(ins) == 2:
        return local_call(invert_pair_kernel, ins, [square, square], scratch, 40 * 10**9, "sum_invert")
    return [ins[0], local_call(invert_kernel, ins, [square], scratch, 40 * 10**9, "invert")[0]]


def join(target, mine, other, index, axis):
    half = mine.shape[axis]
    for value, at in ((mine, index), (other, 1 - index)):
        place = pl.ds(pl.multiple_of(at * half, half), half)
        if axis:
            target[:, place] = value[...]
        else:
            target[place, :] = value[...]


def update_kernel(
    last, diag, low_a, low_b, high_a, high_b, link_a, link_b, next_a, next_b, link_low, right_low, right_high, right,
    new_diag, new_link, new_right, low, high, link, nxt,
):
    index = lax.axis_index("blk")
    half = link_low.shape[1]
    join(low, low_a, low_b, index, 0)
    join(high, high_a, high_b, index, 0)
    join(link, link_a, link_b, index, 1)
    join(nxt, next_a, next_b, index, 1)
    mine = pl.ds(pl.multiple_of(index * half, half), half)
    low_pair = split(low[...])
    high_pair = split(high[...])
    link_pair = split(link[...])
    next_pair = split(nxt[...])
    link_rows = split(link[mine, :]) if last else link_pair
    next_columns = split(nxt[:, mine]) if last else next_pair
    old = diag[:, mine] if last else diag[...]
    gram = split(multiply(low_pair, link_rows, NT))
    upper = split(multiply(high_pair, next_columns))
    new_diag[...] = old + multiply(link_pair, gram) + multiply(next_pair, upper, TN)
    new_link[...] = multiply(link_pair, split(multiply(low_pair, split(link_low[...]))))
    scaled_low = split(multiply(low_pair, split(right_low[...])))
    scaled_high = split(multiply(high_pair, split(right_high[...])))
    new_right[...] = right[...] + multiply(link_pair, scaled_low) + multiply(next_pair, scaled_high, TN)


def shifted(block, axis, distance):
    devices = range(lax.axis_size(axis))
    route = [(i - distance, i) for i in devices if i - distance in devices]
    return lax.ppermute(block, axis, route)


def swapped(block):
    return lax.ppermute(block, "blk", [(0, 1), (1, 0)])


def shards(hessian_part, coupling, rhs):
    order = coupling.shape[1]
    half = coupling.shape[2]
    blk_index = lax.axis_index("blk")
    section_index = lax.axis_index("hor")
    link = coupling[0]
    link = jnp.where(section_index >= 1, link, jnp.zeros_like(link))
    right = rhs[0]
    ins = [hessian_part[0], swapped(hessian_part[0])]
    for depth in range(LEVELS):
        last = depth == LEVELS - 1
        distance = 2**depth
        next_link = shifted(link, "hor", -distance)
        link_low = shifted(link, "hor", distance)
        right_low = shifted(right, "hor", distance)
        right_high = shifted(right, "hor", -distance)
        link_other = swapped(link)
        next_other = swapped(next_link)
        diag, negated = invert(ins, order)
        mine = lax.dynamic_slice_in_dim(negated, blk_index * half, half, 0)
        low = shifted(mine, "hor", distance)
        high = shifted(mine, "hor", -distance)
        low_other = swapped(low)
        high_other = swapped(high)
        square = pltpu.VMEM((order, order), jnp.float32)
        args = [diag, low, low_other, high, high_other, link, link_other, next_link, next_other]
        args += [link_low, right_low, right_high, right]
        shape = (order, half) if last else (order, order)
        diag, link, right = local_call(
            functools.partial(update_kernel, last), args, [shape, (order, half), right.shape], [square] * 4, 3 * 10**9, "update"
        )
        ins = [diag]
    return (diag[None], link[None], right[None])


def solution(mesh):
    spec = P(("grp", "hor"), None, "blk")
    return jax.shard_map(
        shards,
        mesh=mesh,
        in_specs=(P(("grp", "hor"), "blk", None), spec, spec),
        out_specs=(spec, spec, spec),
        check_vma=False,
    )
```

time: 532 us -> 174 us (0.33); the launches traced: 522 us -> 174 us
  other arithmetic: 244 us -> 0.04 us
  waiting for transfers between devices: 148 us -> 48.9 us
  Pallas kernels: 0 us -> 75.6 us
  matrix products: 52.6 us -> 0 us
  local copies, waits for them, and re-layouts: 36.5 us -> 3.08 us
  starting transfers between devices: 12.4 us -> 45.5 us
  between operations: 29.1 us -> 0.86 us
    another operation x34 -> x0, other arithmetic: 238 us -> none  [the longest x29 158 us: shards(): factor = jnp.linalg.cholesky(diag_full)]
    pallas_call x0 -> x4, Pallas kernels: none -> 75.6 us  [local_call(): pl.pallas_call(kernel, out_shape=[jax.ShapeDtypeStruct(s, jnp.float32) fo...]
    ppermute x4 -> x12, waiting for transfers between devices: 121 us -> 47.7 us  [shifted(): return lax.ppermute(block, axis, route)]
    ppermute x4 -> x12, starting transfers between devices: 11.8 us -> 42.9 us  [shifted(): return lax.ppermute(block, axis, route)]
    dot_general x16 -> x0, matrix products: 30.9 us -> none  [product_of(): jnp.dot(left, right, precision=lax.Precision.HIGHEST, preferred_element_t...]
    psum x1 -> x0, waiting for transfers between devices: 21.7 us -> none  [shards(): diag_full = lax.psum(partial_value, 'blk')]
    another operation x26 -> x0, matrix products: 21.7 us -> none  [the longest x12 10.9 us: shards(): factor = jnp.linalg.cholesky(diag_full)]
    another operation x35 -> x0, local copies, waits for them, and re-layouts: 20 us -> none  [the longest x27 19.7 us: shards(): lax.linalg.triangular_solve(factor, identity, left_side=True, lower=True)]
  transfers between devices with their start and end apart: 8 -> 21, of which waited for: 6 -> 6; matrix products, arithmetic and copies ran while one was open for 57% -> 0% of each run, Pallas kernels for 0% -> 34%
where the time goes in v1:
time: 174 us
  Pallas kernels  75.6 us (43%)
  waiting for transfers between devices  48.9 us (28%)
  starting transfers between devices  45.5 us (26%)
  local copies, waits for them, and re-layouts  3.08 us (2%)
    pallas_call x4, Pallas kernels, local_call(): pl.pallas_call(kernel, out_shape=[jax.ShapeDtypeStruct(s, jnp.float32) fo...  75.6 us
    ppermute x12, waiting for transfers between devices, shifted(): return lax.ppermute(block, axis, route)  47.7 us
    ppermute x12, starting transfers between devices, shifted(): return lax.ppermute(block, axis, route)  42.9 us
  transfers between devices with their start and end apart: 21, of which 6 were waited for; matrix products, arithmetic and copies ran while one was open for 0% of the time, Pallas kernels for 34%

profile of v1, /device:TPU:0, one launch (start us, length us, event | category | flops | bytes accessed | tf_op | source)
XLA Modules:
  0.0 174.0 jit_solution(2811526450134213782)
XLA Ops:
  0.6 0.5 collective-permute-start
  1.2 1.3 collective-permute-start.6
  2.5 1.2 collective-permute-done.b_ref
  3.7 29.8 %sum_invert.1 = (f32[512,512]{1,0:T(8,128)S(1)}, f32[512,512]{1,0:T(8,128)S(1)}) custom-call(f32[512,512]{1,0:T(8,128)S(1)} %bitcast.8, f32[512,512]{1,0:T(8,128)S(1)} %collective-permute-done.b_ref), custom_call_target="tpu_custom_call" | custom-call | flops 40000000000 | bytes 4194304 | tf_op jit(solution)/shard_map/sum_invert/pallas_call | solution.py:120
  33.5 1.0 copy-done.3
  34.6 1.4 collective-permute-start.3
  36.0 5.7 %collective-permute-start.1 = (f32[256,512]{1,0:T(8,128)S(1)}, f32[256,512]{1,0:T(8,128)S(1)}, u32[]{:S(2)}, u32[]{:S(2)}) collective-permute-start(f32[256,512]{1,0:T(8,128)S(1)} %constant_dynamic-slice_fusion.1), channel_id=1, source_target_pairs={{0,2},{2,4},{4,6},{6,8},{8,10},{10,12},{12,14},{1,3},{3,5},{5,7},{... | collective-permute-start | bytes 1572872 | tf_op jit(solution)/shard_map/ppermute | solution.py:180
  41.7 1.3 collective-permute-start.10
  43.0 5.4 %collective-permute-start.9 = (f32[512,128]{1,0:T(8,128)S(1)}, f32[512,128]{1,0:T(8,128)S(1)}, u32[]{:S(2)}, u32[]{:S(2)}) collective-permute-start(f32[512,128]{1,0:T(8,128)S(1)} %bitcast.10), channel_id=1, source_target_pairs={{0,2},{2,4},{4,6},{6,8},{8,10},{10,12},{12,14},{1,3},{3,5},{5,7},{... | collective-permute-start | bytes 786440 | tf_op jit(solution)/shard_map/ppermute | solution.py:180
  48.4 9.4 %collective-permute-done.10.right_high = f32[512,128]{1,0:T(8,128)S(1)} collective-permute-done((f32[512,128]{1,0:T(8,128)S(1)}, f32[512,128]{1,0:T(8,128)S(1)}, u32[]{:S(2)}, u32[]{:S(2)}) %collective-permute-start.10) | collective-permute-done | bytes 262176 | tf_op jit(solution)/shard_map/ppermute | solution.py:180
  57.8 4.9 %collective-permute-start.8 = (f32[512,256]{1,0:T(8,128)S(1)}, f32[512,256]{1,0:T(8,128)S(1)}, u32[]{:S(2)}, u32[]{:S(2)}) collective-permute-start(f32[512,256]{1,0:T(8,128)S(1)} %select_bitcast_fusion.link_a), channel_id=1, source_target_pairs={{0,2},{2,4},{4,6},{6,8},{8,10},{10,12},{12,14},{1,3},{3,5},{5,7},{... | collective-permute-start | bytes 1572872 | tf_op jit(solution)/shard_map/ppermute | solution.py:180
  62.7 12.2 %collective-permute-done.9.right_low = f32[512,128]{1,0:T(8,128)S(1)} collective-permute-done((f32[512,128]{1,0:T(8,128)S(1)}, f32[512,128]{1,0:T(8,128)S(1)}, u32[]{:S(2)}, u32[]{:S(2)}) %collective-permute-start.9) | collective-permute-done | bytes 262176 | tf_op jit(solution)/shard_map/ppermute | solution.py:180
  74.9 0.5 collective-permute-start.7
  75.5 0.4 collective-permute-start.2
  75.9 10.2 %collective-permute-done.8.link_low = f32[512,256]{1,0:T(8,128)S(1)} collective-permute-done((f32[512,256]{1,0:T(8,128)S(1)}, f32[512,256]{1,0:T(8,128)S(1)}, u32[]{:S(2)}, u32[]{:S(2)}) %collective-permute-start.8) | collective-permute-done | bytes 524320 | tf_op jit(solution)/shard_map/ppermute | solution.py:180
  86.1 0.8 copy-done.4
  86.9 8.7 %update.2 = (f32[512,512]{1,0:T(8,128)}, f32[512,256]{1,0:T(8,128)S(1)}, f32[512,128]{1,0:T(8,128)S(1)}) custom-call(f32[512,512]{1,0:T(8,128)} %copy-done.3, f32[256,512]{1,0:T(8,128)S(1)} %collective-permute-done.1.low_a, f32[256,512]{1,0:T(8,128)S(1)} %collective-permute-done.2.low_b, f32[256,512]{1,0:T(8,128)S(1)} %collective-permute-done.3.high_a, ...), custom_call_target="tpu_custom_call" | custom-call | flops 3000000000 | bytes 4194304 | tf_op jit(solution)/shard_map/update/pallas_call | solution.py:120
  95.6 1.3 collective-permute-start.16
  96.9 1.2 copy-done.2
  98.1 29.8 %invert.1 = f32[512,512]{1,0:T(8,128)S(1)} custom-call(f32[512,512]{1,0:T(8,128)S(1)} %copy-done.2), custom_call_target="tpu_custom_call" | custom-call | flops 40000000000 | bytes 4194304 | tf_op jit(solution)/shard_map/invert/pallas_call | solution.py:120
  127.9 1.5 collective-permute-start.13
  129.4 10.6 %collective-permute-start.11 = (f32[256,512]{1,0:T(8,128)S(1)}, f32[256,512]{1,0:T(8,128)S(1)}, u32[]{:S(2)}, u32[]{:S(2)}) collective-permute-start(f32[256,512]{1,0:T(8,128)S(1)} %constant_dynamic-slice_fusion), channel_id=1, source_target_pairs={{0,4},{2,6},{4,8},{6,10},{8,12},{10,14},{1,5},{3,7},{5,9},{7,11},{... | collective-permute-start | bytes 1572872 | tf_op jit(solution)/shard_map/ppermute | solution.py:180
  140.1 1.3 collective-permute-start.20
  141.4 4.6 %collective-permute-start.19 = (f32[512,128]{1,0:T(8,128)S(1)}, f32[512,128]{1,0:T(8,128)S(1)}, u32[]{:S(2)}, u32[]{:S(2)}) collective-permute-start(f32[512,128]{1,0:T(8,128)S(1)} %get-tuple-element.15.right), channel_id=1, source_target_pairs={{0,4},{2,6},{4,8},{6,10},{8,12},{10,14},{1,5},{3,7},{5,9},{7,11},{... | collective-permute-start | bytes 786440 | tf_op jit(solution)/shard_map/ppermute | solution.py:180
  145.9 8.1 %collective-permute-done.20.right_high = f32[512,128]{1,0:T(8,128)S(1)} collective-permute-done((f32[512,128]{1,0:T(8,128)S(1)}, f32[512,128]{1,0:T(8,128)S(1)}, u32[]{:S(2)}, u32[]{:S(2)}) %collective-permute-start.20) | collective-permute-done | bytes 262176 | tf_op jit(solution)/shard_map/ppermute | solution.py:180
  154.0 3.7 %collective-permute-start.18 = (f32[512,256]{1,0:T(8,128)S(1)}, f32[512,256]{1,0:T(8,128)S(1)}, u32[]{:S(2)}, u32[]{:S(2)}) collective-permute-start(f32[512,256]{1,0:T(8,128)S(1)} %get-tuple-element.14.link_a), channel_id=1, source_target_pairs={{0,4},{2,6},{4,8},{6,10},{8,12},{10,14},{1,5},{3,7},{5,9},{7,11},{... | collective-permute-start | bytes 1572872 | tf_op jit(solution)/shard_map/ppermute | solution.py:180
  157.7 0.1 collective-permute-start.15
  157.8 0.5 collective-permute-start.17
  158.3 0.1 collective-permute-start.14
  158.3 0.4 collective-permute-start.12
  158.8 7.9 %collective-permute-done.18.link_low = f32[512,256]{1,0:T(8,128)S(1)} collective-permute-done((f32[512,256]{1,0:T(8,128)S(1)}, f32[512,256]{1,0:T(8,128)S(1)}, u32[]{:S(2)}, u32[]{:S(2)}) %collective-permute-start.18) | collective-permute-done | bytes 524320 | tf_op jit(solution)/shard_map/ppermute | solution.py:180
  166.7 7.3 %update.3 = (f32[512,256]{1,0:T(8,128)}, f32[512,256]{1,0:T(8,128)}, f32[512,128]{1,0:T(8,128)}) custom-call(f32[512,512]{1,0:T(8,128)} %get-tuple-element.13.a_ref.diag, f32[256,512]{1,0:T(8,128)S(1)} %collective-permute-done.11.low_a, f32[256,512]{1,0:T(8,128)S(1)} %collective-permute-done.12.low_b, f32[256,512]{1,0:T(8,128)S(1)} %collective-permute-done.13.high_a, ...), custom_call_target="tpu_custom_call" | custom-call | flops 3000000000 | bytes 4194304 | tf_op jit(solution)/shard_map/update/pallas_call | solution.py:120
  (27 shorter events, 0.3 us)
Async XLA Ops:
  0.6 3.0 %copy-start = (f32[1,512,512]{2,1,0:T(8,128)S(1)}, f32[1,512,512]{2,1,0:T(8,128)}, u32[]{:S(2)}) copy-start(f32[1,512,512]{2,1,0:T(8,128)} %param.3) | copy-start | bytes 3145732
  0.6 3.0 %collective-permute-start = (f32[512,512]{1,0:T(8,128)}, f32[512,512]{1,0:T(8,128)S(1)}, u32[]{:S(2)}, u32[]{:S(2)}) collective-permute-start(f32[512,512]{1,0:T(8,128)} %bitcast.7), channel_id=1, source_target_pairs={{0,1},{1,0},{2,3},{3,2},{4,5},{5,4},{6,7},{7,6},{8,9},{9,8},{10,11... | collective-permute-start | bytes 3145736 | tf_op jit(solution)/shard_map/ppermute | solution.py:184
  1.2 73.7 %collective-permute-start.6 = (f32[512,256]{1,0:T(8,128)S(1)}, f32[512,256]{1,0:T(8,128)S(1)}, u32[]{:S(2)}, u32[]{:S(2)}) collective-permute-start(f32[512,256]{1,0:T(8,128)S(1)} %select_bitcast_fusion.link_a), channel_id=1, source_target_pairs={{2,0},{4,2},{6,4},{8,6},{10,8},{12,10},{14,12},{3,1},{5,3},{7,5},{... | collective-permute-start | bytes 1572872 | tf_op jit(solution)/shard_map/ppermute | solution.py:180
  33.5 1.0 copy-start.3
  34.5 7.2 %copy-start.1 = (f32[1,512,128]{2,1,0:T(8,128)S(1)}, f32[1,512,128]{2,1,0:T(8,128)}, u32[]{:S(2)}) copy-start(f32[1,512,128]{2,1,0:T(8,128)} %param.5) | copy-start | bytes 786436
  34.6 40.9 %collective-permute-start.3 = (f32[256,512]{1,0:T(8,128)S(1)}, f32[256,512]{1,0:T(8,128)S(1)}, u32[]{:S(2)}, u32[]{:S(2)}) collective-permute-start(f32[256,512]{1,0:T(8,128)S(1)} %constant_dynamic-slice_fusion.1), channel_id=1, source_target_pairs={{2,0},{4,2},{6,4},{8,6},{10,8},{12,10},{14,12},{3,1},{5,3},{7,5},{... | collective-permute-start | bytes 1572872 | tf_op jit(solution)/shard_map/ppermute | solution.py:180
  36.0 39.5 %collective-permute-start.1 = (f32[256,512]{1,0:T(8,128)S(1)}, f32[256,512]{1,0:T(8,128)S(1)}, u32[]{:S(2)}, u32[]{:S(2)}) collective-permute-start(f32[256,512]{1,0:T(8,128)S(1)} %constant_dynamic-slice_fusion.1), channel_id=1, source_target_pairs={{0,2},{2,4},{4,6},{6,8},{8,10},{10,12},{12,14},{1,3},{3,5},{5,7},{... | collective-permute-start | bytes 1572872 | tf_op jit(solution)/shard_map/ppermute | solution.py:180
  41.7 16.1 %collective-permute-start.10 = (f32[512,128]{1,0:T(8,128)S(1)}, f32[512,128]{1,0:T(8,128)S(1)}, u32[]{:S(2)}, u32[]{:S(2)}) collective-permute-start(f32[512,128]{1,0:T(8,128)S(1)} %bitcast.9), channel_id=1, source_target_pairs={{2,0},{4,2},{6,4},{8,6},{10,8},{12,10},{14,12},{3,1},{5,3},{7,5},{... | collective-permute-start | bytes 786440 | tf_op jit(solution)/shard_map/ppermute | solution.py:180
  43.0 31.9 %collective-permute-start.9 = (f32[512,128]{1,0:T(8,128)S(1)}, f32[512,128]{1,0:T(8,128)S(1)}, u32[]{:S(2)}, u32[]{:S(2)}) collective-permute-start(f32[512,128]{1,0:T(8,128)S(1)} %bitcast.10), channel_id=1, source_target_pairs={{0,2},{2,4},{4,6},{6,8},{8,10},{10,12},{12,14},{1,3},{3,5},{5,7},{... | collective-permute-start | bytes 786440 | tf_op jit(solution)/shard_map/ppermute | solution.py:180
  57.8 28.3 %collective-permute-start.8 = (f32[512,256]{1,0:T(8,128)S(1)}, f32[512,256]{1,0:T(8,128)S(1)}, u32[]{:S(2)}, u32[]{:S(2)}) collective-permute-start(f32[512,256]{1,0:T(8,128)S(1)} %select_bitcast_fusion.link_a), channel_id=1, source_target_pairs={{0,2},{2,4},{4,6},{6,8},{8,10},{10,12},{12,14},{1,3},{3,5},{5,7},{... | collective-permute-start | bytes 1572872 | tf_op jit(solution)/shard_map/ppermute | solution.py:180
  74.9 11.2 %collective-permute-start.5 = (f32[512,256]{1,0:T(8,128)S(1)}, f32[512,256]{1,0:T(8,128)S(1)}, u32[]{:S(2)}, u32[]{:S(2)}) collective-permute-start(f32[512,256]{1,0:T(8,128)S(1)} %select_bitcast_fusion.link_a), channel_id=1, source_target_pairs={{0,1},{1,0},{2,3},{3,2},{4,5},{5,4},{6,7},{7,6},{8,9},{9,8},{10,11... | collective-permute-start | bytes 1572872 | tf_op jit(solution)/shard_map/ppermute | solution.py:184
  74.9 11.2 %collective-permute-start.7 = (f32[512,256]{1,0:T(8,128)S(1)}, f32[512,256]{1,0:T(8,128)S(1)}, u32[]{:S(2)}, u32[]{:S(2)}) collective-permute-start(f32[512,256]{1,0:T(8,128)S(1)} %collective-permute-done.6.next_a), channel_id=1, source_target_pairs={{0,1},{1,0},{2,3},{3,2},{4,5},{5,4},{6,7},{7,6},{8,9},{9,8},{10,11... | collective-permute-start | bytes 1572872 | tf_op jit(solution)/shard_map/ppermute | solution.py:184
  75.4 10.7 %collective-permute-start.4 = (f32[256,512]{1,0:T(8,128)S(1)}, f32[256,512]{1,0:T(8,128)S(1)}, u32[]{:S(2)}, u32[]{:S(2)}) collective-permute-start(f32[256,512]{1,0:T(8,128)S(1)} %collective-permute-done.3.high_a), channel_id=1, source_target_pairs={{0,1},{1,0},{2,3},{3,2},{4,5},{5,4},{6,7},{7,6},{8,9},{9,8},{10,11... | collective-permute-start | bytes 1572872 | tf_op jit(solution)/shard_map/ppermute | solution.py:184
  75.5 10.6 %collective-permute-start.2 = (f32[256,512]{1,0:T(8,128)S(1)}, f32[256,512]{1,0:T(8,128)S(1)}, u32[]{:S(2)}, u32[]{:S(2)}) collective-permute-start(f32[256,512]{1,0:T(8,128)S(1)} %collective-permute-done.1.low_a), channel_id=1, source_target_pairs={{0,1},{1,0},{2,3},{3,2},{4,5},{5,4},{6,7},{7,6},{8,9},{9,8},{10,11... | collective-permute-start | bytes 1572872 | tf_op jit(solution)/shard_map/ppermute | solution.py:184
  86.1 0.8 copy-start.4
  95.6 62.2 %collective-permute-start.16 = (f32[512,256]{1,0:T(8,128)S(1)}, f32[512,256]{1,0:T(8,128)S(1)}, u32[]{:S(2)}, u32[]{:S(2)}) collective-permute-start(f32[512,256]{1,0:T(8,128)S(1)} %get-tuple-element.14.link_a), channel_id=1, source_target_pairs={{4,0},{6,2},{8,4},{10,6},{12,8},{14,10},{5,1},{7,3},{9,5},{11,7},{... | collective-permute-start | bytes 1572872 | tf_op jit(solution)/shard_map/ppermute | solution.py:180
  96.9 1.2 copy-start.2
  127.9 30.4 %collective-permute-start.13 = (f32[256,512]{1,0:T(8,128)S(1)}, f32[256,512]{1,0:T(8,128)S(1)}, u32[]{:S(2)}, u32[]{:S(2)}) collective-permute-start(f32[256,512]{1,0:T(8,128)S(1)} %constant_dynamic-slice_fusion), channel_id=1, source_target_pairs={{4,0},{6,2},{8,4},{10,6},{12,8},{14,10},{5,1},{7,3},{9,5},{11,7},{... | collective-permute-start | bytes 1572872 | tf_op jit(solution)/shard_map/ppermute | solution.py:180
  129.4 28.9 %collective-permute-start.11 = (f32[256,512]{1,0:T(8,128)S(1)}, f32[256,512]{1,0:T(8,128)S(1)}, u32[]{:S(2)}, u32[]{:S(2)}) collective-permute-start(f32[256,512]{1,0:T(8,128)S(1)} %constant_dynamic-slice_fusion), channel_id=1, source_target_pairs={{0,4},{2,6},{4,8},{6,10},{8,12},{10,14},{1,5},{3,7},{5,9},{7,11},{... | collective-permute-start | bytes 1572872 | tf_op jit(solution)/shard_map/ppermute | solution.py:180
  140.1 13.9 %collective-permute-start.20 = (f32[512,128]{1,0:T(8,128)S(1)}, f32[512,128]{1,0:T(8,128)S(1)}, u32[]{:S(2)}, u32[]{:S(2)}) collective-permute-start(f32[512,128]{1,0:T(8,128)S(1)} %get-tuple-element.15.right), channel_id=1, source_target_pairs={{4,0},{6,2},{8,4},{10,6},{12,8},{14,10},{5,1},{7,3},{9,5},{11,7},{... | collective-permute-start | bytes 786440 | tf_op jit(solution)/shard_map/ppermute | solution.py:180
  141.4 16.3 %collective-permute-start.19 = (f32[512,128]{1,0:T(8,128)S(1)}, f32[512,128]{1,0:T(8,128)S(1)}, u32[]{:S(2)}, u32[]{:S(2)}) collective-permute-start(f32[512,128]{1,0:T(8,128)S(1)} %get-tuple-element.15.right), channel_id=1, source_target_pairs={{0,4},{2,6},{4,8},{6,10},{8,12},{10,14},{1,5},{3,7},{5,9},{7,11},{... | collective-permute-start | bytes 786440 | tf_op jit(solution)/shard_map/ppermute | solution.py:180
  154.0 12.6 %collective-permute-start.18 = (f32[512,256]{1,0:T(8,128)S(1)}, f32[512,256]{1,0:T(8,128)S(1)}, u32[]{:S(2)}, u32[]{:S(2)}) collective-permute-start(f32[512,256]{1,0:T(8,128)S(1)} %get-tuple-element.14.link_a), channel_id=1, source_target_pairs={{0,4},{2,6},{4,8},{6,10},{8,12},{10,14},{1,5},{3,7},{5,9},{7,11},{... | collective-permute-start | bytes 1572872 | tf_op jit(solution)/shard_map/ppermute | solution.py:180
  157.7 9.0 %collective-permute-start.15 = (f32[512,256]{1,0:T(8,128)S(1)}, f32[512,256]{1,0:T(8,128)S(1)}, u32[]{:S(2)}, u32[]{:S(2)}) collective-permute-start(f32[512,256]{1,0:T(8,128)S(1)} %get-tuple-element.14.link_a), channel_id=1, source_target_pairs={{0,1},{1,0},{2,3},{3,2},{4,5},{5,4},{6,7},{7,6},{8,9},{9,8},{10,11... | collective-permute-start | bytes 1572872 | tf_op jit(solution)/shard_map/ppermute | solution.py:184
  157.8 8.9 %collective-permute-start.17 = (f32[512,256]{1,0:T(8,128)S(1)}, f32[512,256]{1,0:T(8,128)S(1)}, u32[]{:S(2)}, u32[]{:S(2)}) collective-permute-start(f32[512,256]{1,0:T(8,128)S(1)} %collective-permute-done.16.next_a), channel_id=1, source_target_pairs={{0,1},{1,0},{2,3},{3,2},{4,5},{5,4},{6,7},{7,6},{8,9},{9,8},{10,11... | collective-permute-start | bytes 1572872 | tf_op jit(solution)/shard_map/ppermute | solution.py:184
  158.3 8.4 %collective-permute-start.14 = (f32[256,512]{1,0:T(8,128)S(1)}, f32[256,512]{1,0:T(8,128)S(1)}, u32[]{:S(2)}, u32[]{:S(2)}) collective-permute-start(f32[256,512]{1,0:T(8,128)S(1)} %collective-permute-done.13.high_a), channel_id=1, source_target_pairs={{0,1},{1,0},{2,3},{3,2},{4,5},{5,4},{6,7},{7,6},{8,9},{9,8},{10,11... | collective-permute-start | bytes 1572872 | tf_op jit(solution)/shard_map/ppermute | solution.py:184
  158.3 8.3 %collective-permute-start.12 = (f32[256,512]{1,0:T(8,128)S(1)}, f32[256,512]{1,0:T(8,128)S(1)}, u32[]{:S(2)}, u32[]{:S(2)}) collective-permute-start(f32[256,512]{1,0:T(8,128)S(1)} %collective-permute-done.11.low_a), channel_id=1, source_target_pairs={{0,1},{1,0},{2,3},{3,2},{4,5},{5,4},{6,7},{7,6},{8,9},{9,8},{10,11... | collective-permute-start | bytes 1572872 | tf_op jit(solution)/shard_map/ppermute | solution.py:184

commit v2 on v1

--- a/solution.py
+++ b/solution.py
@@ -100,17 +100,48 @@
     lax.fori_loop(0, order // BASE, step, 0)
 
 
+def lower_blocks(order):
+    count = order // BASE
+    return [(i, j) for i in range(count) for j in range(i + 1)]
+
+
+def pack_half(out_ref, work):
+    blocks = lower_blocks(work.shape[0])
+    half = len(blocks) // 2
+    first = lax.axis_index("blk") == 0
+    for n in range(half):
+        (i, j), (k, l) = blocks[n], blocks[half + n]
+        mine = work[i * BASE : (i + 1) * BASE, j * BASE : (j + 1) * BASE]
+        other = work[k * BASE : (k + 1) * BASE, l * BASE : (l + 1) * BASE]
+        out_ref[n * BASE : (n + 1) * BASE, :] = jnp.where(first, mine, other)
+
+
 def invert_pair_kernel(a_ref, b_ref, total_ref, out_ref, work, base):
     total_ref[...] = a_ref[...] + b_ref[...]
     work[...] = total_ref[...]
     sweep_all(work, base)
-    out_ref[...] = work[...]
+    pack_half(out_ref, work)
 
 
 def invert_kernel(a_ref, out_ref, work, base):
     work[...] = a_ref[...]
     sweep_all(work, base)
-    out_ref[...] = work[...]
+    pack_half(out_ref, work)
+
+
+def gate_kernel(*refs):
+    pass
+
+
+def gated(packed, others):
+    return pl.pallas_call(
+        gate_kernel,
+        out_shape=jax.ShapeDtypeStruct(packed.shape, packed.dtype),
+        in_specs=[pl.BlockSpec(memory_space=pl.ANY)] * (1 + len(others)),
+        out_specs=pl.BlockSpec(memory_space=pl.ANY),
+        input_output_aliases={0: 0},
+        name="gate",
+    )(packed, *others)
 
 
 VMEM = pl.BlockSpec(memory_space=pltpu.VMEM)
@@ -132,19 +163,27 @@
 def invert(ins, order):
     scratch = [pltpu.VMEM((order, order), jnp.float32), pltpu.VMEM((BASE, BASE), jnp.float32)]
     square = (order, order)
+    packed = (len(lower_blocks(order)) // 2 * BASE, BASE)
     if len(ins) == 2:
-        return local_call(invert_pair_kernel, ins, [square, square], scratch, 40 * 10**9, "sum_invert")
-    return [ins[0], local_call(invert_kernel, ins, [square], scratch, 40 * 10**9, "invert")[0]]
-
-
-def join(target, mine, other, index, axis):
-    half = mine.shape[axis]
+        return local_call(invert_pair_kernel, ins, [square, packed], scratch, 40 * 10**9, "sum_invert")
+    return [ins[0], local_call(invert_kernel, ins, [packed], scratch, 40 * 10**9, "invert")[0]]
+
+
+def join(target, mine, other, index):
+    half = mine.shape[1]
     for value, at in ((mine, index), (other, 1 - index)):
-        place = pl.ds(pl.multiple_of(at * half, half), half)
-        if axis:
-            target[:, place] = value[...]
-        else:
-            target[place, :] = value[...]
+        target[:, pl.ds(pl.multiple_of(at * half, half), half)] = value[...]
+
+
+def unpack(target, mine, other, index):
+    blocks = lower_blocks(target.shape[0])
+    half = len(blocks) // 2
+    for n, (i, j) in enumerate(blocks):
+        place = slice(n % half * BASE, (n % half + 1) * BASE)
+        block = jnp.where(index == n // half, mine[place, :], other[place, :])
+        target[i * BASE : (i + 1) * BASE, j * BASE : (j + 1) * BASE] = block
+        if i != j:
+            target[j * BASE : (j + 1) * BASE, i * BASE : (i + 1) * BASE] = block.T
 
 
 def update_kernel(
@@ -153,10 +192,10 @@
 ):
     index = lax.axis_index("blk")
     half = link_low.shape[1]
-    join(low, low_a, low_b, index, 0)
-    join(high, high_a, high_b, index, 0)
-    join(link, link_a, link_b, index, 1)
-    join(nxt, next_a, next_b, index, 1)
+    unpack(low, low_a, low_b, index)
+    unpack(high, high_a, high_b, index)
+    join(link, link_a, link_b, index)
+    join(nxt, next_a, next_b, index)
     mine = pl.ds(pl.multiple_of(index * half, half), half)
     low_pair = split(low[...])
     high_pair = split(high[...])
@@ -187,7 +226,6 @@
 def shards(hessian_part, coupling, rhs):
     order = coupling.shape[1]
     half = coupling.shape[2]
-    blk_index = lax.axis_index("blk")
     section_index = lax.axis_index("hor")
     link = coupling[0]
     link = jnp.where(section_index >= 1, link, jnp.zeros_like(link))
@@ -202,8 +240,8 @@
         right_high = shifted(right, "hor", -distance)
         link_other = swapped(link)
         next_other = swapped(next_link)
-        diag, negated = invert(ins, order)
-        mine = lax.dynamic_slice_in_dim(negated, blk_index * half, half, 0)
+        diag, mine = invert(ins, order)
+        mine = gated(mine, [next_link, link_low, right_low, right_high, link_other])
         low = shifted(mine, "hor", distance)
         high = shifted(mine, "hor", -distance)
         low_other = swapped(low)

time: 174 us -> 158 us (0.908)
  waiting for transfers between devices: 48.9 us -> 23.6 us
  local copies, waits for them, and re-layouts: 3.08 us -> 18 us
  starting transfers between devices: 45.5 us -> 39 us
    ppermute x12, waiting for transfers between devices: 47.7 us -> 20.3 us  [shifted(): return lax.ppermute(block, axis, route)]
    unnamed x10 -> x54, local copies, waits for them, and re-layouts: 3 us -> 18 us
    ppermute x12, starting transfers between devices: 42.9 us -> 38 us  [shifted(): return lax.ppermute(block, axis, route)]
    ppermute x9, waiting for transfers between devices: 1.17 us -> 3.24 us  [swapped(): return lax.ppermute(block, 'blk', [(0, 1), (1, 0)])]
  transfers between devices with their start and end apart: 21 -> 21, of which waited for: 6 -> 7; matrix products, arithmetic and copies ran while one was open for 0% -> 0% of each run, Pallas kernels for 34% -> 39%
where the time goes in v2:
time: 158 us; the launch traced here: 157 us
  Pallas kernels  75.1 us (48%)
  starting transfers between devices  39 us (25%)
  waiting for transfers between devices  23.6 us (15%)
  local copies, waits for them, and re-layouts  18 us (11%)
    pallas_call x4, Pallas kernels, local_call(): pl.pallas_call(kernel, out_shape=[jax.ShapeDtypeStruct(s, jnp.float32) fo...  75.1 us
    ppermute x12, starting transfers between devices, shifted(): return lax.ppermute(block, axis, route)  38 us
    ppermute x12, waiting for transfers between devices, shifted(): return lax.ppermute(block, axis, route)  20.3 us
    unnamed x54, local copies, waits for them, and re-layouts  18 us
    ppermute x9, waiting for transfers between devices, swapped(): return lax.ppermute(block, 'blk', [(0, 1), (1, 0)])  3.24 us
  transfers between devices with their start and end apart: 21, of which 7 were waited for; matrix products, arithmetic and copies ran while one was open for 0% of the time, Pallas kernels for 39%

profile of v2, /device:TPU:0, one launch (start us, length us, event | category | flops | bytes accessed | tf_op | source)
XLA Modules:
  0.0 156.7 jit_solution(1362913722040662488)
XLA Ops:
  1.1 1.3 collective-permute-start.4
  2.4 5.1 %collective-permute-start.3 = (f32[512,128]{1,0:T(8,128)}, f32[512,128]{1,0:T(8,128)S(1)}, u32[]{:S(2)}, u32[]{:S(2)}) collective-permute-start(f32[512,128]{1,0:T(8,128)} %bitcast.10), channel_id=1, source_target_pairs={{0,2},{2,4},{4,6},{6,8},{8,10},{10,12},{12,14},{1,3},{3,5},{5,7},{... | collective-permute-start | bytes 786440 | tf_op jit(solution)/shard_map/ppermute | solution.py:219
  7.8 5.8 %collective-permute-start.2 = (f32[512,256]{1,0:T(8,128)S(1)}, f32[512,256]{1,0:T(8,128)S(1)}, u32[]{:S(2)}, u32[]{:S(2)}) collective-permute-start(f32[512,256]{1,0:T(8,128)S(1)} %select_bitcast_fusion.link_a), channel_id=1, source_target_pairs={{0,2},{2,4},{4,6},{6,8},{8,10},{10,12},{12,14},{1,3},{3,5},{5,7},{... | collective-permute-start | bytes 1572872 | tf_op jit(solution)/shard_map/ppermute | solution.py:219
  13.6 1.3 collective-permute-start.1
  14.9 31.0 %sum_invert.1 = (f32[512,512]{1,0:T(8,128)S(1)}, f32[640,128]{1,0:T(8,128)S(1)}) custom-call(f32[512,512]{1,0:T(8,128)S(1)} %bitcast.8, f32[512,512]{1,0:T(8,128)} %collective-permute-done.b_ref), custom_call_target="tpu_custom_call" | custom-call | flops 40000000000 | bytes 4194304 | tf_op jit(solution)/shard_map/sum_invert/pallas_call | solution.py:151
  46.7 1.0 copy-done.26
  49.0 1.4 collective-permute-start.8
  50.4 5.4 %collective-permute-start.6 = (f32[640,128]{1,0:T(8,128)}, f32[640,128]{1,0:T(8,128)S(1)}, u32[]{:S(2)}, u32[]{:S(2)}) collective-permute-start(f32[640,128]{1,0:T(8,128)} %gate.2), channel_id=1, source_target_pairs={{0,2},{2,4},{4,6},{6,8},{8,10},{10,12},{12,14},{1,3},{3,5},{5,7},{... | collective-permute-start | bytes 983048 | tf_op jit(solution)/shard_map/ppermute | solution.py:219
  55.9 5.8 %collective-permute-done.8.high_a = f32[640,128]{1,0:T(8,128)S(1)} collective-permute-done((f32[640,128]{1,0:T(8,128)}, f32[640,128]{1,0:T(8,128)S(1)}, u32[]{:S(2)}, u32[]{:S(2)}) %collective-permute-start.8) | collective-permute-done | bytes 327712 | tf_op jit(solution)/shard_map/ppermute | solution.py:219
  61.7 7.3 %collective-permute-done.6.low_a = f32[640,128]{1,0:T(8,128)S(1)} collective-permute-done((f32[640,128]{1,0:T(8,128)}, f32[640,128]{1,0:T(8,128)S(1)}, u32[]{:S(2)}, u32[]{:S(2)}) %collective-permute-start.6) | collective-permute-done | bytes 327712 | tf_op jit(solution)/shard_map/ppermute | solution.py:219
  69.0 1.6 %collective-permute-done.7.low_b = f32[640,128]{1,0:T(8,128)S(1)} collective-permute-done((f32[640,128]{1,0:T(8,128)S(1)}, f32[640,128]{1,0:T(8,128)S(1)}, u32[]{:S(2)}, u32[]{:S(2)}) %collective-permute-start.7) | collective-permute-done | bytes 327712 | tf_op jit(solution)/shard_map/ppermute | solution.py:223
  70.6 1.0 copy-done.1
  71.6 1.0 copy-done.3
  72.7 1.0 copy-done.9
  73.7 0.9 copy-done.15
  75.6 8.3 %update.2 = (f32[512,512]{1,0:T(8,128)}, f32[512,256]{1,0:T(8,128)S(1)}, f32[512,128]{1,0:T(8,128)S(1)}) custom-call(f32[512,512]{1,0:T(8,128)} %copy-done.26, f32[640,128]{1,0:T(8,128)S(1)} %collective-permute-done.6.low_a, f32[640,128]{1,0:T(8,128)S(1)} %collective-permute-done.7.low_b, f32[640,128]{1,0:T(8,128)S(1)} %collective-permute-done.8.high_a, ...), custom_call_target="tpu_custom_call" | custom-call | flops 3000000000 | bytes 4194304 | tf_op jit(solution)/shard_map/update/pallas_call | solution.py:151
  84.0 1.3 collective-permute-start.14
  85.3 4.6 %collective-permute-start.13 = (f32[512,128]{1,0:T(8,128)S(1)}, f32[512,128]{1,0:T(8,128)S(1)}, u32[]{:S(2)}, u32[]{:S(2)}) collective-permute-start(f32[512,128]{1,0:T(8,128)S(1)} %get-tuple-element.15.right), channel_id=1, source_target_pairs={{0,4},{2,6},{4,8},{6,10},{8,12},{10,14},{1,5},{3,7},{5,9},{7,11},{... | collective-permute-start | bytes 786440 | tf_op jit(solution)/shard_map/ppermute | solution.py:219
  89.9 3.9 %collective-permute-start.12 = (f32[512,256]{1,0:T(8,128)S(1)}, f32[512,256]{1,0:T(8,128)S(1)}, u32[]{:S(2)}, u32[]{:S(2)}) collective-permute-start(f32[512,256]{1,0:T(8,128)S(1)} %get-tuple-element.14.link_a), channel_id=1, source_target_pairs={{0,4},{2,6},{4,8},{6,10},{8,12},{10,14},{1,5},{3,7},{5,9},{7,11},{... | collective-permute-start | bytes 1572872 | tf_op jit(solution)/shard_map/ppermute | solution.py:219
  93.9 1.5 collective-permute-start.11
  95.4 1.2 copy-done.24
  96.6 29.7 %invert.1.refs_0_ = f32[640,128]{1,0:T(8,128)S(1)} custom-call(f32[512,512]{1,0:T(8,128)S(1)} %copy-done.24), custom_call_target="tpu_custom_call" | custom-call | flops 40000000000 | bytes 4194304 | tf_op jit(solution)/shard_map/invert/pallas_call | solution.py:151
  129.0 1.3 collective-permute-start.18
  130.3 5.2 %collective-permute-start.16 = (f32[640,128]{1,0:T(8,128)}, f32[640,128]{1,0:T(8,128)S(1)}, u32[]{:S(2)}, u32[]{:S(2)}) collective-permute-start(f32[640,128]{1,0:T(8,128)} %gate.3), channel_id=1, source_target_pairs={{0,4},{2,6},{4,8},{6,10},{8,12},{10,14},{1,5},{3,7},{5,9},{7,11},{... | collective-permute-start | bytes 983048 | tf_op jit(solution)/shard_map/ppermute | solution.py:219
  135.6 6.0 %collective-permute-done.18.high_a = f32[640,128]{1,0:T(8,128)S(1)} collective-permute-done((f32[640,128]{1,0:T(8,128)}, f32[640,128]{1,0:T(8,128)S(1)}, u32[]{:S(2)}, u32[]{:S(2)}) %collective-permute-start.18) | collective-permute-done | bytes 327712 | tf_op jit(solution)/shard_map/ppermute | solution.py:219
  141.6 1.3 collective-permute-done.16.low_a
  143.2 1.3 collective-permute-done.17.low_b
  144.5 1.0 copy-done.5
  145.5 1.0 copy-done.7
  146.6 1.0 copy-done.11
  149.5 1.2 copy-done.25
  150.7 6.0 %update.3 = (f32[512,256]{1,0:T(8,128)}, f32[512,256]{1,0:T(8,128)}, f32[512,128]{1,0:T(8,128)}) custom-call(f32[512,512]{1,0:T(8,128)S(1)} %copy-done.25, f32[640,128]{1,0:T(8,128)S(1)} %collective-permute-done.16.low_a, f32[640,128]{1,0:T(8,128)S(1)} %collective-permute-done.17.low_b, f32[640,128]{1,0:T(8,128)S(1)} %collective-permute-done.18.high_a, ...), custom_call_target="tpu_custom_call" | custom-call | flops 3000000000 | bytes 4194304 | tf_op jit(solution)/shard_map/update/pallas_call | solution.py:151
  (71 shorter events, 8.9 us)
Async XLA Ops:
  0.6 13.0 %collective-permute-start = (f32[512,512]{1,0:T(8,128)}, f32[512,512]{1,0:T(8,128)}, u32[]{:S(2)}, u32[]{:S(2)}) collective-permute-start(f32[512,512]{1,0:T(8,128)} %bitcast.7), channel_id=1, source_target_pairs={{0,1},{1,0},{2,3},{3,2},{4,5},{5,4},{6,7},{7,6},{8,9},{9,8},{10,11... | collective-permute-start | bytes 3145736 | tf_op jit(solution)/shard_map/ppermute | solution.py:223
  1.1 46.6 %collective-permute-start.4 = (f32[512,128]{1,0:T(8,128)}, f32[512,128]{1,0:T(8,128)S(1)}, u32[]{:S(2)}, u32[]{:S(2)}) collective-permute-start(f32[512,128]{1,0:T(8,128)} %bitcast.9), channel_id=1, source_target_pairs={{2,0},{4,2},{6,4},{8,6},{10,8},{12,10},{14,12},{3,1},{5,3},{7,5},{... | collective-permute-start | bytes 786440 | tf_op jit(solution)/shard_map/ppermute | solution.py:219
  2.4 45.3 %collective-permute-start.3 = (f32[512,128]{1,0:T(8,128)}, f32[512,128]{1,0:T(8,128)S(1)}, u32[]{:S(2)}, u32[]{:S(2)}) collective-permute-start(f32[512,128]{1,0:T(8,128)} %bitcast.10), channel_id=1, source_target_pairs={{0,2},{2,4},{4,6},{6,8},{8,10},{10,12},{12,14},{1,3},{3,5},{5,7},{... | collective-permute-start | bytes 786440 | tf_op jit(solution)/shard_map/ppermute | solution.py:219
  7.5 7.4 %copy-start.22 = (f32[1,512,512]{2,1,0:T(8,128)S(1)}, f32[1,512,512]{2,1,0:T(8,128)}, u32[]{:S(2)}) copy-start(f32[1,512,512]{2,1,0:T(8,128)} %param.3) | copy-start | bytes 3145732
  7.6 40.2 %collective-permute-start.5 = (f32[512,256]{1,0:T(8,128)S(1)}, f32[512,256]{1,0:T(8,128)S(1)}, u32[]{:S(2)}, u32[]{:S(2)}) collective-permute-start(f32[512,256]{1,0:T(8,128)S(1)} %select_bitcast_fusion.link_a), channel_id=1, source_target_pairs={{0,1},{1,0},{2,3},{3,2},{4,5},{5,4},{6,7},{7,6},{8,9},{9,8},{10,11... | collective-permute-start | bytes 1572872 | tf_op jit(solution)/shard_map/ppermute | solution.py:223
  7.8 39.9 %collective-permute-start.2 = (f32[512,256]{1,0:T(8,128)S(1)}, f32[512,256]{1,0:T(8,128)S(1)}, u32[]{:S(2)}, u32[]{:S(2)}) collective-permute-start(f32[512,256]{1,0:T(8,128)S(1)} %select_bitcast_fusion.link_a), channel_id=1, source_target_pairs={{0,2},{2,4},{4,6},{6,8},{8,10},{10,12},{12,14},{1,3},{3,5},{5,7},{... | collective-permute-start | bytes 1572872 | tf_op jit(solution)/shard_map/ppermute | solution.py:219
  13.6 34.1 %collective-permute-start.1 = (f32[512,256]{1,0:T(8,128)S(1)}, f32[512,256]{1,0:T(8,128)S(1)}, u32[]{:S(2)}, u32[]{:S(2)}) collective-permute-start(f32[512,256]{1,0:T(8,128)S(1)} %select_bitcast_fusion.link_a), channel_id=1, source_target_pairs={{2,0},{4,2},{6,4},{8,6},{10,8},{12,10},{14,12},{3,1},{5,3},{7,5},{... | collective-permute-start | bytes 1572872 | tf_op jit(solution)/shard_map/ppermute | solution.py:219
  47.8 1.1 copy-start.2
  47.8 1.2 copy-start.8
  49.0 21.6 %copy-start.23 = (f32[1,512,128]{2,1,0:T(8,128)S(1)}, f32[1,512,128]{2,1,0:T(8,128)}, u32[]{:S(2)}) copy-start(f32[1,512,128]{2,1,0:T(8,128)} %param.5) | copy-start | bytes 786436
  49.0 12.7 %collective-permute-start.8 = (f32[640,128]{1,0:T(8,128)}, f32[640,128]{1,0:T(8,128)S(1)}, u32[]{:S(2)}, u32[]{:S(2)}) collective-permute-start(f32[640,128]{1,0:T(8,128)} %gate.2), channel_id=1, source_target_pairs={{2,0},{4,2},{6,4},{8,6},{10,8},{12,10},{14,12},{3,1},{5,3},{7,5},{... | collective-permute-start | bytes 983048 | tf_op jit(solution)/shard_map/ppermute | solution.py:219
  50.4 18.5 %collective-permute-start.6 = (f32[640,128]{1,0:T(8,128)}, f32[640,128]{1,0:T(8,128)S(1)}, u32[]{:S(2)}, u32[]{:S(2)}) collective-permute-start(f32[640,128]{1,0:T(8,128)} %gate.2), channel_id=1, source_target_pairs={{0,2},{2,4},{4,6},{6,8},{8,10},{10,12},{12,14},{1,3},{3,5},{5,7},{... | collective-permute-start | bytes 983048 | tf_op jit(solution)/shard_map/ppermute | solution.py:219
  55.8 13.2 %collective-permute-start.10 = (f32[512,256]{1,0:T(8,128)}, f32[512,256]{1,0:T(8,128)S(1)}, u32[]{:S(2)}, u32[]{:S(2)}) collective-permute-start(f32[512,256]{1,0:T(8,128)} %copy-done.8), channel_id=1, source_target_pairs={{0,1},{1,0},{2,3},{3,2},{4,5},{5,4},{6,7},{7,6},{8,9},{9,8},{10,11... | collective-permute-start | bytes 1572872 | tf_op jit(solution)/shard_map/ppermute | solution.py:223
  61.7 7.3 %collective-permute-start.9 = (f32[640,128]{1,0:T(8,128)S(1)}, f32[640,128]{1,0:T(8,128)S(1)}, u32[]{:S(2)}, u32[]{:S(2)}) collective-permute-start(f32[640,128]{1,0:T(8,128)S(1)} %collective-permute-done.8.high_a), channel_id=1, source_target_pairs={{0,1},{1,0},{2,3},{3,2},{4,5},{5,4},{6,7},{7,6},{8,9},{9,8},{10,11... | collective-permute-start | bytes 983048 | tf_op jit(solution)/shard_map/ppermute | solution.py:223
  69.0 1.6 %collective-permute-start.7 = (f32[640,128]{1,0:T(8,128)S(1)}, f32[640,128]{1,0:T(8,128)S(1)}, u32[]{:S(2)}, u32[]{:S(2)}) collective-permute-start(f32[640,128]{1,0:T(8,128)S(1)} %collective-permute-done.6.low_a), channel_id=1, source_target_pairs={{0,1},{1,0},{2,3},{3,2},{4,5},{5,4},{6,7},{7,6},{8,9},{9,8},{10,11... | collective-permute-start | bytes 983048 | tf_op jit(solution)/shard_map/ppermute | solution.py:223
  70.6 1.0 copy-start.1
  71.6 1.0 copy-start.3
  72.7 1.0 copy-start.9
  84.0 43.1 %collective-permute-start.14 = (f32[512,128]{1,0:T(8,128)S(1)}, f32[512,128]{1,0:T(8,128)S(1)}, u32[]{:S(2)}, u32[]{:S(2)}) collective-permute-start(f32[512,128]{1,0:T(8,128)S(1)} %get-tuple-element.15.right), channel_id=1, source_target_pairs={{4,0},{6,2},{8,4},{10,6},{12,8},{14,10},{5,1},{7,3},{9,5},{11,7},{... | collective-permute-start | bytes 786440 | tf_op jit(solution)/shard_map/ppermute | solution.py:219
  85.3 41.8 %collective-permute-start.13 = (f32[512,128]{1,0:T(8,128)S(1)}, f32[512,128]{1,0:T(8,128)S(1)}, u32[]{:S(2)}, u32[]{:S(2)}) collective-permute-start(f32[512,128]{1,0:T(8,128)S(1)} %get-tuple-element.15.right), channel_id=1, source_target_pairs={{0,4},{2,6},{4,8},{6,10},{8,12},{10,14},{1,5},{3,7},{5,9},{7,11},{... | collective-permute-start | bytes 786440 | tf_op jit(solution)/shard_map/ppermute | solution.py:219
  89.8 37.3 %collective-permute-start.15 = (f32[512,256]{1,0:T(8,128)S(1)}, f32[512,256]{1,0:T(8,128)S(1)}, u32[]{:S(2)}, u32[]{:S(2)}) collective-permute-start(f32[512,256]{1,0:T(8,128)S(1)} %get-tuple-element.14.link_a), channel_id=1, source_target_pairs={{0,1},{1,0},{2,3},{3,2},{4,5},{5,4},{6,7},{7,6},{8,9},{9,8},{10,11... | collective-permute-start | bytes 1572872 | tf_op jit(solution)/shard_map/ppermute | solution.py:223
  89.9 37.2 %collective-permute-start.12 = (f32[512,256]{1,0:T(8,128)S(1)}, f32[512,256]{1,0:T(8,128)S(1)}, u32[]{:S(2)}, u32[]{:S(2)}) collective-permute-start(f32[512,256]{1,0:T(8,128)S(1)} %get-tuple-element.14.link_a), channel_id=1, source_target_pairs={{0,4},{2,6},{4,8},{6,10},{8,12},{10,14},{1,5},{3,7},{5,9},{7,11},{... | collective-permute-start | bytes 1572872 | tf_op jit(solution)/shard_map/ppermute | solution.py:219
  93.9 33.3 %collective-permute-start.11 = (f32[512,256]{1,0:T(8,128)S(1)}, f32[512,256]{1,0:T(8,128)S(1)}, u32[]{:S(2)}, u32[]{:S(2)}) collective-permute-start(f32[512,256]{1,0:T(8,128)S(1)} %get-tuple-element.14.link_a), channel_id=1, source_target_pairs={{4,0},{6,2},{8,4},{10,6},{12,8},{14,10},{5,1},{7,3},{9,5},{11,7},{... | collective-permute-start | bytes 1572872 | tf_op jit(solution)/shard_map/ppermute | solution.py:219
  95.4 1.2 copy-start.24
  127.1 1.1 copy-start.6
  129.0 12.5 %collective-permute-start.18 = (f32[640,128]{1,0:T(8,128)}, f32[640,128]{1,0:T(8,128)S(1)}, u32[]{:S(2)}, u32[]{:S(2)}) collective-permute-start(f32[640,128]{1,0:T(8,128)} %gate.3), channel_id=1, source_target_pairs={{4,0},{6,2},{8,4},{10,6},{12,8},{14,10},{5,1},{7,3},{9,5},{11,7},{... | collective-permute-start | bytes 983048 | tf_op jit(solution)/shard_map/ppermute | solution.py:219
  130.3 12.5 %collective-permute-start.16 = (f32[640,128]{1,0:T(8,128)}, f32[640,128]{1,0:T(8,128)S(1)}, u32[]{:S(2)}, u32[]{:S(2)}) collective-permute-start(f32[640,128]{1,0:T(8,128)} %gate.3), channel_id=1, source_target_pairs={{0,4},{2,6},{4,8},{6,10},{8,12},{10,14},{1,5},{3,7},{5,9},{7,11},{... | collective-permute-start | bytes 983048 | tf_op jit(solution)/shard_map/ppermute | solution.py:219
  135.5 7.3 %collective-permute-start.20 = (f32[512,256]{1,0:T(8,128)}, f32[512,256]{1,0:T(8,128)S(1)}, u32[]{:S(2)}, u32[]{:S(2)}) collective-permute-start(f32[512,256]{1,0:T(8,128)} %copy-done.10), channel_id=1, source_target_pairs={{0,1},{1,0},{2,3},{3,2},{4,5},{5,4},{6,7},{7,6},{8,9},{9,8},{10,11... | collective-permute-start | bytes 1572872 | tf_op jit(solution)/shard_map/ppermute | solution.py:223
  141.5 1.6 %collective-permute-start.19 = (f32[640,128]{1,0:T(8,128)S(1)}, f32[640,128]{1,0:T(8,128)S(1)}, u32[]{:S(2)}, u32[]{:S(2)}) collective-permute-start(f32[640,128]{1,0:T(8,128)S(1)} %collective-permute-done.18.high_a), channel_id=1, source_target_pairs={{0,1},{1,0},{2,3},{3,2},{4,5},{5,4},{6,7},{7,6},{8,9},{9,8},{10,11... | collective-permute-start | bytes 983048 | tf_op jit(solution)/shard_map/ppermute | solution.py:223
  142.8 1.6 %collective-permute-start.17 = (f32[640,128]{1,0:T(8,128)S(1)}, f32[640,128]{1,0:T(8,128)S(1)}, u32[]{:S(2)}, u32[]{:S(2)}) collective-permute-start(f32[640,128]{1,0:T(8,128)S(1)} %collective-permute-done.16.low_a), channel_id=1, source_target_pairs={{0,1},{1,0},{2,3},{3,2},{4,5},{5,4},{6,7},{7,6},{8,9},{9,8},{10,11... | collective-permute-start | bytes 983048 | tf_op jit(solution)/shard_map/ppermute | solution.py:223
  144.5 1.0 copy-start.5
  149.5 1.2 copy-start.25
  (16 other events, 14.0 us)

commit v3 on v2

--- a/solution.py
+++ b/solution.py
@@ -35,10 +35,11 @@
         first = p * ROWS
         block = tiles[p]
         columns = [
-            [jnp.broadcast_to(tiles[q][:, first + l : first + l + 1], shape) for l in range(ROWS)] for q in range(count)
+            [jnp.broadcast_to(tiles[q][:, first + l : first + l + 1], shape) for l in range(ROWS)]
+            for q in range(p, min(p + 2, count))
         ]
         e = {
-            (i, j): jnp.broadcast_to(columns[p][j][i : i + 1, :], shape) for i in range(ROWS) for j in range(i + 1)
+            (i, j): jnp.broadcast_to(columns[0][j][i : i + 1, :], shape) for i in range(ROWS) for j in range(i + 1)
         }
         at = lambda i, j: (max(i, j), min(i, j))
         for k in range(ROWS):
@@ -67,12 +68,19 @@
             rows = jnp.where(lane == first + l, negated[l], rows)
         spread = [jnp.broadcast_to(rows[l : l + 1, :], shape) for l in range(ROWS)]
         inside = (lane >= first) & (lane < first + ROWS)
+        panel = jnp.concatenate([jnp.where(inside, tile, 0.0) for tile in tiles], 0)
+        zero = jnp.zeros(shape, jnp.float32)
+        padded = jnp.concatenate([rows if q == p else zero for q in range(count)], 0)
+        delta = multiply(split(panel), split(padded))
         for q in range(count):
             if q == p:
                 continue
             value = jnp.where(inside, 0.0, tiles[q])
-            for l in range(ROWS):
-                value = value - columns[q][l] * spread[l]
+            if q == p + 1:
+                for l in range(ROWS):
+                    value = value - columns[1][l] * spread[l]
+            else:
+                value = value - delta[q * ROWS : (q + 1) * ROWS, :]
             tiles[q] = value
         tiles[p] = rows
     return tiles
@@ -147,14 +155,14 @@
 VMEM = pl.BlockSpec(memory_space=pltpu.VMEM)
 
 
-def local_call(kernel, ins, outs, scratch, flops, name):
+def local_call(kernel, ins, outs, scratch, flops, name, mib):
     return pl.pallas_call(
         kernel,
         out_shape=[jax.ShapeDtypeStruct(s, jnp.float32) for s in outs],
         in_specs=[VMEM] * len(ins),
         out_specs=[VMEM] * len(outs),
         scratch_shapes=scratch,
-        compiler_params=pltpu.CompilerParams(vmem_limit_bytes=48 * 2**20),
+        compiler_params=pltpu.CompilerParams(vmem_limit_bytes=mib * 2**20),
         cost_estimate=pl.CostEstimate(flops=flops, bytes_accessed=4 * 2**20, transcendentals=0),
         name=name,
     )(*ins)
@@ -165,8 +173,8 @@
     square = (order, order)
     packed = (len(lower_blocks(order)) // 2 * BASE, BASE)
     if len(ins) == 2:
-        return local_call(invert_pair_kernel, ins, [square, packed], scratch, 40 * 10**9, "sum_invert")
-    return [ins[0], local_call(invert_kernel, ins, [packed], scratch, 40 * 10**9, "invert")[0]]
+        return local_call(invert_pair_kernel, ins, [square, packed], scratch, 40 * 10**9, "sum_invert", 20)
+    return [ins[0], local_call(invert_kernel, ins, [packed], scratch, 40 * 10**9, "invert", 20)[0]]
 
 
 def join(target, mine, other, index):
@@ -186,16 +194,14 @@
             target[j * BASE : (j + 1) * BASE, i * BASE : (i + 1) * BASE] = block.T
 
 
-def update_kernel(
-    last, diag, low_a, low_b, high_a, high_b, link_a, link_b, next_a, next_b, link_low, right_low, right_high, right,
-    new_diag, new_link, new_right, low, high, link, nxt,
-):
+def update_kernel(last, diag, low_a, low_b, high_a, high_b, both, link_b, both_low, both_high, next_b, new_diag, *rest):
+    *new_both, low, high, link, nxt = rest
     index = lax.axis_index("blk")
-    half = link_low.shape[1]
+    half = link_b.shape[1]
     unpack(low, low_a, low_b, index)
     unpack(high, high_a, high_b, index)
-    join(link, link_a, link_b, index)
-    join(nxt, next_a, next_b, index)
+    join(link, both[:, :half], link_b, index)
+    join(nxt, both_high[:, :half], next_b, index)
     mine = pl.ds(pl.multiple_of(index * half, half), half)
     low_pair = split(low[...])
     high_pair = split(high[...])
@@ -207,10 +213,15 @@
     gram = split(multiply(low_pair, link_rows, NT))
     upper = split(multiply(high_pair, next_columns))
     new_diag[...] = old + multiply(link_pair, gram) + multiply(next_pair, upper, TN)
-    new_link[...] = multiply(link_pair, split(multiply(low_pair, split(link_low[...]))))
-    scaled_low = split(multiply(low_pair, split(right_low[...])))
-    scaled_high = split(multiply(high_pair, split(right_high[...])))
-    new_right[...] = right[...] + multiply(link_pair, scaled_low) + multiply(next_pair, scaled_high, TN)
+    from_low = multiply(link_pair, split(multiply(low_pair, split(both_low[...]))))
+    scaled_high = split(multiply(high_pair, split(both_high[:, half:])))
+    right = both[:, half:] + from_low[:, half:] + multiply(next_pair, scaled_high, TN)
+    if last:
+        new_both[0][...] = from_low[:, :half]
+        new_both[1][...] = right
+    else:
+        new_both[0][:, :half] = from_low[:, :half]
+        new_both[0][:, half:] = right
 
 
 def shifted(block, axis, distance):
@@ -229,32 +240,28 @@
     section_index = lax.axis_index("hor")
     link = coupling[0]
     link = jnp.where(section_index >= 1, link, jnp.zeros_like(link))
-    right = rhs[0]
+    both = jnp.concatenate([link, rhs[0]], 1)
+    width = both.shape[1]
     ins = [hessian_part[0], swapped(hessian_part[0])]
     for depth in range(LEVELS):
         last = depth == LEVELS - 1
         distance = 2**depth
-        next_link = shifted(link, "hor", -distance)
-        link_low = shifted(link, "hor", distance)
-        right_low = shifted(right, "hor", distance)
-        right_high = shifted(right, "hor", -distance)
-        link_other = swapped(link)
-        next_other = swapped(next_link)
+        both_low = shifted(both, "hor", distance)
+        both_high = shifted(both, "hor", -distance)
         diag, mine = invert(ins, order)
-        mine = gated(mine, [next_link, link_low, right_low, right_high, link_other])
+        mine = gated(mine, [both_low, both_high])
+        link_other = swapped(both[:, :half])
+        next_other = swapped(both_high[:, :half])
         low = shifted(mine, "hor", distance)
         high = shifted(mine, "hor", -distance)
         low_other = swapped(low)
         high_other = swapped(high)
         square = pltpu.VMEM((order, order), jnp.float32)
-        args = [diag, low, low_other, high, high_other, link, link_other, next_link, next_other]
-        args += [link_low, right_low, right_high, right]
-        shape = (order, half) if last else (order, order)
-        diag, link, right = local_call(
-            functools.partial(update_kernel, last), args, [shape, (order, half), right.shape], [square] * 4, 3 * 10**9, "update"
-        )
-        ins = [diag]
-    return (diag[None], link[None], right[None])
+        args = [diag, low, low_other, high, high_other, both, link_other, both_low, both_high, next_other]
+        outs = [(order, half), (order, half), (order, width - half)] if last else [(order, order), (order, width)]
+        diag, *rest = local_call(functools.partial(update_kernel, last), args, outs, [square] * 4, 3 * 10**9, "update", 32)
+        ins, both = [diag], rest[0]
+    return (diag[None], rest[0][None], rest[1][None])
 
 
 def solution(mesh):

time: 158 us -> 124 us (0.78)
  Pallas kernels: 75.1 us -> 52.4 us
  starting transfers between devices: 39 us -> 27.6 us
  waiting for transfers between devices: 23.6 us -> 32.9 us
  local copies, waits for them, and re-layouts: 18 us -> 9.56 us
    pallas_call x4, Pallas kernels: 75.1 us -> 52.4 us  [local_call(): pl.pallas_call(kernel, out_shape=[jax.ShapeDtypeStruct(s, jnp.float32) fo...]
    ppermute x12 -> x8, starting transfers between devices: 38 us -> 25.8 us  [shifted(): return lax.ppermute(block, axis, route)]
    unnamed x54 -> x32, local copies, waits for them, and re-layouts: 18 us -> 8.41 us
    ppermute x12 -> x8, waiting for transfers between devices: 20.3 us -> 29.7 us  [shifted(): return lax.ppermute(block, axis, route)]
  transfers between devices with their start and end apart: 21 -> 17, of which waited for: 7 -> 8; matrix products, arithmetic and copies ran while one was open for 0% -> 1% of each run, Pallas kernels for 39% -> 32%
where the time goes in v3:
time: 124 us; the launch traced here: 123 us
  Pallas kernels  52.4 us (42%)
  waiting for transfers between devices  32.9 us (27%)
  starting transfers between devices  27.6 us (22%)
  local copies, waits for them, and re-layouts  9.56 us (8%)
    pallas_call x4, Pallas kernels, local_call(): pl.pallas_call(kernel, out_shape=[jax.ShapeDtypeStruct(s, jnp.float32) fo...  52.4 us
    ppermute x8, waiting for transfers between devices, shifted(): return lax.ppermute(block, axis, route)  29.7 us
    ppermute x8, starting transfers between devices, shifted(): return lax.ppermute(block, axis, route)  25.8 us
    unnamed x32, local copies, waits for them, and re-layouts  8.41 us
    ppermute x9, waiting for transfers between devices, swapped(): return lax.ppermute(block, 'blk', [(0, 1), (1, 0)])  3.22 us
  transfers between devices with their start and end apart: 17, of which 8 were waited for; matrix products, arithmetic and copies ran while one was open for 1% of the time, Pallas kernels for 32%

profile of v3, /device:TPU:0, one launch (start us, length us, event | category | flops | bytes accessed | tf_op | source)
XLA Modules:
  0.0 123.4 jit_solution(5759123266377479045)
XLA Ops:
  0.6 0.5 collective-permute-start
  1.2 0.8 copy-done.13
  2.2 1.3 %collective-permute-start.2 = (f32[512,384]{1,0:T(8,128)S(1)}, f32[512,384]{1,0:T(8,128)S(1)}, u32[]{:S(2)}, u32[]{:S(2)}) collective-permute-start(f32[512,384]{1,0:T(8,128)S(1)} %pad_maximum_fusion.both), channel_id=1, source_target_pairs={{2,0},{4,2},{6,4},{8,6},{10,8},{12,10},{14,12},{3,1},{5,3},{7,5},{... | collective-permute-start | bytes 2359304 | tf_op jit(solution)/shard_map/ppermute | solution.py:230
  3.5 6.1 %collective-permute-start.1 = (f32[512,384]{1,0:T(8,128)S(1)}, f32[512,384]{1,0:T(8,128)S(1)}, u32[]{:S(2)}, u32[]{:S(2)}) collective-permute-start(f32[512,384]{1,0:T(8,128)S(1)} %pad_maximum_fusion.both), channel_id=1, source_target_pairs={{0,2},{2,4},{4,6},{6,8},{8,10},{10,12},{12,14},{1,3},{3,5},{5,7},{... | collective-permute-start | bytes 2359304 | tf_op jit(solution)/shard_map/ppermute | solution.py:230
  9.6 19.6 %sum_invert.1 = (f32[512,512]{1,0:T(8,128)S(1)}, f32[640,128]{1,0:T(8,128)S(1)}) custom-call(f32[512,512]{1,0:T(8,128)S(1)} %bitcast.8, f32[512,512]{1,0:T(8,128)S(1)} %collective-permute-done.b_ref), custom_call_target="tpu_custom_call" | custom-call | flops 40000000000 | bytes 4194304 | tf_op jit(solution)/shard_map/sum_invert/pallas_call | solution.py:159
  29.1 0.7 copy-done.8
  29.9 1.0 copy-done.11
  30.8 11.9 %collective-permute-done.1.refs_1_.both_low = f32[512,384]{1,0:T(8,128)S(1)} collective-permute-done((f32[512,384]{1,0:T(8,128)S(1)}, f32[512,384]{1,0:T(8,128)S(1)}, u32[]{:S(2)}, u32[]{:S(2)}) %collective-permute-start.1) | collective-permute-done | bytes 786464 | tf_op jit(solution)/shard_map/ppermute | solution.py:230
  42.8 0.9 copy-done.4
  43.7 1.4 %collective-permute-start.5 = (f32[640,128]{1,0:T(8,128)}, f32[640,128]{1,0:T(8,128)S(1)}, u32[]{:S(2)}, u32[]{:S(2)}) collective-permute-start(f32[640,128]{1,0:T(8,128)} %gate.2), channel_id=1, source_target_pairs={{2,0},{4,2},{6,4},{8,6},{10,8},{12,10},{14,12},{3,1},{5,3},{7,5},{... | collective-permute-start | bytes 983048 | tf_op jit(solution)/shard_map/ppermute | solution.py:230
  45.1 5.0 %collective-permute-start.3 = (f32[640,128]{1,0:T(8,128)}, f32[640,128]{1,0:T(8,128)S(1)}, u32[]{:S(2)}, u32[]{:S(2)}) collective-permute-start(f32[640,128]{1,0:T(8,128)} %gate.2), channel_id=1, source_target_pairs={{0,2},{2,4},{4,6},{6,8},{8,10},{10,12},{12,14},{1,3},{3,5},{5,7},{... | collective-permute-start | bytes 983048 | tf_op jit(solution)/shard_map/ppermute | solution.py:230
  50.2 1.1 slice.12
  51.3 0.6 collective-permute-start.8
  51.8 4.5 %collective-permute-done.5.high_a = f32[640,128]{1,0:T(8,128)S(1)} collective-permute-done((f32[640,128]{1,0:T(8,128)}, f32[640,128]{1,0:T(8,128)S(1)}, u32[]{:S(2)}, u32[]{:S(2)}) %collective-permute-start.5) | collective-permute-done | bytes 327712 | tf_op jit(solution)/shard_map/ppermute | solution.py:230
  56.3 7.3 %collective-permute-done.3.low_a = f32[640,128]{1,0:T(8,128)S(1)} collective-permute-done((f32[640,128]{1,0:T(8,128)}, f32[640,128]{1,0:T(8,128)S(1)}, u32[]{:S(2)}, u32[]{:S(2)}) %collective-permute-start.3) | collective-permute-done | bytes 327712 | tf_op jit(solution)/shard_map/ppermute | solution.py:230
  63.6 1.6 %collective-permute-done.4.low_b = f32[640,128]{1,0:T(8,128)S(1)} collective-permute-done((f32[640,128]{1,0:T(8,128)S(1)}, f32[640,128]{1,0:T(8,128)S(1)}, u32[]{:S(2)}, u32[]{:S(2)}) %collective-permute-start.4) | collective-permute-done | bytes 327712 | tf_op jit(solution)/shard_map/ppermute | solution.py:234
  65.2 1.1 copy-done.5
  66.4 1.2 copy-done.12
  67.6 7.2 %update.2 = (f32[512,512]{1,0:T(8,128)S(1)}, f32[512,384]{1,0:T(8,128)S(1)}) custom-call(f32[512,512]{1,0:T(8,128)S(1)} %copy-done.12, f32[640,128]{1,0:T(8,128)S(1)} %collective-permute-done.3.low_a, f32[640,128]{1,0:T(8,128)S(1)} %collective-permute-done.4.low_b, f32[640,128]{1,0:T(8,128)S(1)} %collective-permute-done.5.high_a, ...), custom_call_target="tpu_custom_call" | custom-call | flops 3000000000 | bytes 4194304 | tf_op jit(solution)/shard_map/update/pallas_call | solution.py:159
  74.8 1.3 %collective-permute-start.10 = (f32[512,384]{1,0:T(8,128)S(1)}, f32[512,384]{1,0:T(8,128)S(1)}, u32[]{:S(2)}, u32[]{:S(2)}) collective-permute-start(f32[512,384]{1,0:T(8,128)S(1)} %get-tuple-element.13.both), channel_id=1, source_target_pairs={{4,0},{6,2},{8,4},{10,6},{12,8},{14,10},{5,1},{7,3},{9,5},{11,7},{... | collective-permute-start | bytes 2359304 | tf_op jit(solution)/shard_map/ppermute | solution.py:230
  76.1 4.8 %collective-permute-start.9 = (f32[512,384]{1,0:T(8,128)S(1)}, f32[512,384]{1,0:T(8,128)S(1)}, u32[]{:S(2)}, u32[]{:S(2)}) collective-permute-start(f32[512,384]{1,0:T(8,128)S(1)} %get-tuple-element.13.both), channel_id=1, source_target_pairs={{0,4},{2,6},{4,8},{6,10},{8,12},{10,14},{1,5},{3,7},{5,9},{7,11},{... | collective-permute-start | bytes 2359304 | tf_op jit(solution)/shard_map/ppermute | solution.py:230
  80.9 19.5 %invert.1.refs_0_ = f32[640,128]{1,0:T(8,128)S(1)} custom-call(f32[512,512]{1,0:T(8,128)S(1)} %get-tuple-element.12.a_ref.diag), custom_call_target="tpu_custom_call" | custom-call | flops 40000000000 | bytes 4194304 | tf_op jit(solution)/shard_map/invert/pallas_call | solution.py:159
  100.4 0.7 copy-done.9
  101.1 0.9 copy-done.2
  102.0 0.9 copy-done.6
  102.9 1.4 %collective-permute-start.13 = (f32[640,128]{1,0:T(8,128)}, f32[640,128]{1,0:T(8,128)S(1)}, u32[]{:S(2)}, u32[]{:S(2)}) collective-permute-start(f32[640,128]{1,0:T(8,128)} %gate.3), channel_id=1, source_target_pairs={{4,0},{6,2},{8,4},{10,6},{12,8},{14,10},{5,1},{7,3},{9,5},{11,7},{... | collective-permute-start | bytes 983048 | tf_op jit(solution)/shard_map/ppermute | solution.py:230
  104.3 4.6 %collective-permute-start.11 = (f32[640,128]{1,0:T(8,128)}, f32[640,128]{1,0:T(8,128)S(1)}, u32[]{:S(2)}, u32[]{:S(2)}) collective-permute-start(f32[640,128]{1,0:T(8,128)} %gate.3), channel_id=1, source_target_pairs={{0,4},{2,6},{4,8},{6,10},{8,12},{10,14},{1,5},{3,7},{5,9},{7,11},{... | collective-permute-start | bytes 983048 | tf_op jit(solution)/shard_map/ppermute | solution.py:230
  109.1 0.6 collective-permute-start.16
  109.7 4.7 %collective-permute-done.13.high_a = f32[640,128]{1,0:T(8,128)S(1)} collective-permute-done((f32[640,128]{1,0:T(8,128)}, f32[640,128]{1,0:T(8,128)S(1)}, u32[]{:S(2)}, u32[]{:S(2)}) %collective-permute-start.13) | collective-permute-done | bytes 327712 | tf_op jit(solution)/shard_map/ppermute | solution.py:230
  114.4 1.3 %collective-permute-done.11.low_a = f32[640,128]{1,0:T(8,128)S(1)} collective-permute-done((f32[640,128]{1,0:T(8,128)}, f32[640,128]{1,0:T(8,128)S(1)}, u32[]{:S(2)}, u32[]{:S(2)}) %collective-permute-start.11) | collective-permute-done | bytes 327712 | tf_op jit(solution)/shard_map/ppermute | solution.py:230
  116.0 1.3 %collective-permute-done.12.low_b = f32[640,128]{1,0:T(8,128)S(1)} collective-permute-done((f32[640,128]{1,0:T(8,128)S(1)}, f32[640,128]{1,0:T(8,128)S(1)}, u32[]{:S(2)}, u32[]{:S(2)}) %collective-permute-start.12) | collective-permute-done | bytes 327712 | tf_op jit(solution)/shard_map/ppermute | solution.py:234
  117.3 6.1 %update.3 = (f32[512,256]{1,0:T(8,128)}, f32[512,256]{1,0:T(8,128)}, f32[512,128]{1,0:T(8,128)}) custom-call(f32[512,512]{1,0:T(8,128)S(1)} %get-tuple-element.12.a_ref.diag, f32[640,128]{1,0:T(8,128)S(1)} %collective-permute-done.11.low_a, f32[640,128]{1,0:T(8,128)S(1)} %collective-permute-done.12.low_b, f32[640,128]{1,0:T(8,128)S(1)} %collective-permute-done.13.high_a, ...), custom_call_target="tpu_custom_call" | custom-call | flops 3000000000 | bytes 4194304 | tf_op jit(solution)/shard_map/update/pallas_call | solution.py:159
  (45 shorter events, 0.9 us)
Async XLA Ops:
  0.6 8.9 %collective-permute-start = (f32[512,512]{1,0:T(8,128)}, f32[512,512]{1,0:T(8,128)S(1)}, u32[]{:S(2)}, u32[]{:S(2)}) collective-permute-start(f32[512,512]{1,0:T(8,128)} %bitcast.7), channel_id=1, source_target_pairs={{0,1},{1,0},{2,3},{3,2},{4,5},{5,4},{6,7},{7,6},{8,9},{9,8},{10,11... | collective-permute-start | bytes 3145736 | tf_op jit(solution)/shard_map/ppermute | solution.py:234
  1.1 1.0 copy-start.15
  1.2 0.8 copy-start.13
  1.2 8.3 %copy-start.10 = (f32[1,512,512]{2,1,0:T(8,128)S(1)}, f32[1,512,512]{2,1,0:T(8,128)}, u32[]{:S(2)}) copy-start(f32[1,512,512]{2,1,0:T(8,128)} %param.3) | copy-start | bytes 3145732
  2.2 28.7 %collective-permute-start.2 = (f32[512,384]{1,0:T(8,128)S(1)}, f32[512,384]{1,0:T(8,128)S(1)}, u32[]{:S(2)}, u32[]{:S(2)}) collective-permute-start(f32[512,384]{1,0:T(8,128)S(1)} %pad_maximum_fusion.both), channel_id=1, source_target_pairs={{2,0},{4,2},{6,4},{8,6},{10,8},{12,10},{14,12},{3,1},{5,3},{7,5},{... | collective-permute-start | bytes 2359304 | tf_op jit(solution)/shard_map/ppermute | solution.py:230
  3.5 39.3 %collective-permute-start.1 = (f32[512,384]{1,0:T(8,128)S(1)}, f32[512,384]{1,0:T(8,128)S(1)}, u32[]{:S(2)}, u32[]{:S(2)}) collective-permute-start(f32[512,384]{1,0:T(8,128)S(1)} %pad_maximum_fusion.both), channel_id=1, source_target_pairs={{0,2},{2,4},{4,6},{6,8},{8,10},{10,12},{12,14},{1,3},{3,5},{5,7},{... | collective-permute-start | bytes 2359304 | tf_op jit(solution)/shard_map/ppermute | solution.py:230
  29.1 0.7 copy-start.8
  29.9 1.0 copy-start.11
  30.8 11.9 %copy-start = (f32[512,384]{1,0:T(8,128)}, f32[512,384]{1,0:T(8,128)S(1)}, u32[]{:S(2)}) copy-start(f32[512,384]{1,0:T(8,128)S(1)} %collective-permute-done.2.refs_2_.both_high) | copy-start | bytes 2359300
  42.8 0.9 copy-start.4
  43.7 6.4 %copy-start.14 = (f32[512,256]{1,0:T(8,128)S(1)}, f32[512,256]{1,0:T(8,128)}, u32[]{:S(2)}) copy-start(f32[512,256]{1,0:T(8,128)} %copy-done.13) | copy-start | bytes 1572868
  43.7 21.5 %copy-start.1 = (f32[512,384]{1,0:T(8,128)S(1)}, f32[512,384]{1,0:T(8,128)}, u32[]{:S(2)}) copy-start(f32[512,384]{1,0:T(8,128)} %copy-done) | copy-start | bytes 2359300
  43.7 12.6 %collective-permute-start.5 = (f32[640,128]{1,0:T(8,128)}, f32[640,128]{1,0:T(8,128)S(1)}, u32[]{:S(2)}, u32[]{:S(2)}) collective-permute-start(f32[640,128]{1,0:T(8,128)} %gate.2), channel_id=1, source_target_pairs={{2,0},{4,2},{6,4},{8,6},{10,8},{12,10},{14,12},{3,1},{5,3},{7,5},{... | collective-permute-start | bytes 983048 | tf_op jit(solution)/shard_map/ppermute | solution.py:230
  45.1 18.5 %collective-permute-start.3 = (f32[640,128]{1,0:T(8,128)}, f32[640,128]{1,0:T(8,128)S(1)}, u32[]{:S(2)}, u32[]{:S(2)}) collective-permute-start(f32[640,128]{1,0:T(8,128)} %gate.2), channel_id=1, source_target_pairs={{0,2},{2,4},{4,6},{6,8},{8,10},{10,12},{12,14},{1,3},{3,5},{5,7},{... | collective-permute-start | bytes 983048 | tf_op jit(solution)/shard_map/ppermute | solution.py:230
  50.1 13.5 %collective-permute-start.7 = (f32[512,256]{1,0:T(8,128)S(1)}, f32[512,256]{1,0:T(8,128)S(1)}, u32[]{:S(2)}, u32[]{:S(2)}) collective-permute-start(f32[512,256]{1,0:T(8,128)S(1)} %copy-done.14), channel_id=1, source_target_pairs={{0,1},{1,0},{2,3},{3,2},{4,5},{5,4},{6,7},{7,6},{8,9},{9,8},{10,11... | collective-permute-start | bytes 1572872 | tf_op jit(solution)/shard_map/ppermute | solution.py:234
  51.3 12.3 %collective-permute-start.8 = (f32[512,256]{1,0:T(8,128)S(1)}, f32[512,256]{1,0:T(8,128)S(1)}, u32[]{:S(2)}, u32[]{:S(2)}) collective-permute-start(f32[512,256]{1,0:T(8,128)S(1)} %slice.12), channel_id=1, source_target_pairs={{0,1},{1,0},{2,3},{3,2},{4,5},{5,4},{6,7},{7,6},{8,9},{9,8},{10,11... | collective-permute-start | bytes 1572872 | tf_op jit(solution)/shard_map/ppermute | solution.py:234
  56.3 7.3 %collective-permute-start.6 = (f32[640,128]{1,0:T(8,128)S(1)}, f32[640,128]{1,0:T(8,128)S(1)}, u32[]{:S(2)}, u32[]{:S(2)}) collective-permute-start(f32[640,128]{1,0:T(8,128)S(1)} %collective-permute-done.5.high_a), channel_id=1, source_target_pairs={{0,1},{1,0},{2,3},{3,2},{4,5},{5,4},{6,7},{7,6},{8,9},{9,8},{10,11... | collective-permute-start | bytes 983048 | tf_op jit(solution)/shard_map/ppermute | solution.py:234
  63.6 1.6 %collective-permute-start.4 = (f32[640,128]{1,0:T(8,128)S(1)}, f32[640,128]{1,0:T(8,128)S(1)}, u32[]{:S(2)}, u32[]{:S(2)}) collective-permute-start(f32[640,128]{1,0:T(8,128)S(1)} %collective-permute-done.3.low_a), channel_id=1, source_target_pairs={{0,1},{1,0},{2,3},{3,2},{4,5},{5,4},{6,7},{7,6},{8,9},{9,8},{10,11... | collective-permute-start | bytes 983048 | tf_op jit(solution)/shard_map/ppermute | solution.py:234
  65.2 1.1 copy-start.5
  66.4 1.2 copy-start.12
  74.8 26.3 %collective-permute-start.10 = (f32[512,384]{1,0:T(8,128)S(1)}, f32[512,384]{1,0:T(8,128)S(1)}, u32[]{:S(2)}, u32[]{:S(2)}) collective-permute-start(f32[512,384]{1,0:T(8,128)S(1)} %get-tuple-element.13.both), channel_id=1, source_target_pairs={{4,0},{6,2},{8,4},{10,6},{12,8},{14,10},{5,1},{7,3},{9,5},{11,7},{... | collective-permute-start | bytes 2359304 | tf_op jit(solution)/shard_map/ppermute | solution.py:230
  76.1 25.0 %collective-permute-start.9 = (f32[512,384]{1,0:T(8,128)S(1)}, f32[512,384]{1,0:T(8,128)S(1)}, u32[]{:S(2)}, u32[]{:S(2)}) collective-permute-start(f32[512,384]{1,0:T(8,128)S(1)} %get-tuple-element.13.both), channel_id=1, source_target_pairs={{0,4},{2,6},{4,8},{6,10},{8,12},{10,14},{1,5},{3,7},{5,9},{7,11},{... | collective-permute-start | bytes 2359304 | tf_op jit(solution)/shard_map/ppermute | solution.py:230
  101.1 0.9 copy-start.2
  102.0 0.9 copy-start.6
  102.9 6.1 %copy-start.3 = (f32[512,384]{1,0:T(8,128)S(1)}, f32[512,384]{1,0:T(8,128)}, u32[]{:S(2)}) copy-start(f32[512,384]{1,0:T(8,128)} %copy-done.2) | copy-start | bytes 2359300
  102.9 11.4 %collective-permute-start.13 = (f32[640,128]{1,0:T(8,128)}, f32[640,128]{1,0:T(8,128)S(1)}, u32[]{:S(2)}, u32[]{:S(2)}) collective-permute-start(f32[640,128]{1,0:T(8,128)} %gate.3), channel_id=1, source_target_pairs={{4,0},{6,2},{8,4},{10,6},{12,8},{14,10},{5,1},{7,3},{9,5},{11,7},{... | collective-permute-start | bytes 983048 | tf_op jit(solution)/shard_map/ppermute | solution.py:230
  104.3 11.3 %collective-permute-start.11 = (f32[640,128]{1,0:T(8,128)}, f32[640,128]{1,0:T(8,128)S(1)}, u32[]{:S(2)}, u32[]{:S(2)}) collective-permute-start(f32[640,128]{1,0:T(8,128)} %gate.3), channel_id=1, source_target_pairs={{0,4},{2,6},{4,8},{6,10},{8,12},{10,14},{1,5},{3,7},{5,9},{7,11},{... | collective-permute-start | bytes 983048 | tf_op jit(solution)/shard_map/ppermute | solution.py:230
  109.0 8.3 %copy-start.7 = (f32[512,384]{1,0:T(8,128)S(1)}, f32[512,384]{1,0:T(8,128)}, u32[]{:S(2)}) copy-start(f32[512,384]{1,0:T(8,128)} %copy-done.6) | copy-start | bytes 2359300
  109.0 6.7 %collective-permute-start.15 = (f32[512,256]{1,0:T(8,128)S(1)}, f32[512,256]{1,0:T(8,128)S(1)}, u32[]{:S(2)}, u32[]{:S(2)}) collective-permute-start(f32[512,256]{1,0:T(8,128)S(1)} %slice.10), channel_id=1, source_target_pairs={{0,1},{1,0},{2,3},{3,2},{4,5},{5,4},{6,7},{7,6},{8,9},{9,8},{10,11... | collective-permute-start | bytes 1572872 | tf_op jit(solution)/shard_map/ppermute | solution.py:234
  109.1 6.6 %collective-permute-start.16 = (f32[512,256]{1,0:T(8,128)S(1)}, f32[512,256]{1,0:T(8,128)S(1)}, u32[]{:S(2)}, u32[]{:S(2)}) collective-permute-start(f32[512,256]{1,0:T(8,128)S(1)} %slice.13), channel_id=1, source_target_pairs={{0,1},{1,0},{2,3},{3,2},{4,5},{5,4},{6,7},{7,6},{8,9},{9,8},{10,11... | collective-permute-start | bytes 1572872 | tf_op jit(solution)/shard_map/ppermute | solution.py:234
  114.4 1.6 %collective-permute-start.14 = (f32[640,128]{1,0:T(8,128)S(1)}, f32[640,128]{1,0:T(8,128)S(1)}, u32[]{:S(2)}, u32[]{:S(2)}) collective-permute-start(f32[640,128]{1,0:T(8,128)S(1)} %collective-permute-done.13.high_a), channel_id=1, source_target_pairs={{0,1},{1,0},{2,3},{3,2},{4,5},{5,4},{6,7},{7,6},{8,9},{9,8},{10,11... | collective-permute-start | bytes 983048 | tf_op jit(solution)/shard_map/ppermute | solution.py:234
  115.7 1.6 %collective-permute-start.12 = (f32[640,128]{1,0:T(8,128)S(1)}, f32[640,128]{1,0:T(8,128)S(1)}, u32[]{:S(2)}, u32[]{:S(2)}) collective-permute-start(f32[640,128]{1,0:T(8,128)S(1)} %collective-permute-done.11.low_a), channel_id=1, source_target_pairs={{0,1},{1,0},{2,3},{3,2},{4,5},{5,4},{6,7},{7,6},{8,9},{9,8},{10,11... | collective-permute-start | bytes 983048 | tf_op jit(solution)/shard_map/ppermute | solution.py:234
  (1 other events, 0.7 us)

commit v4 on v3

--- a/solution.py
+++ b/solution.py
@@ -113,28 +113,22 @@
     return [(i, j) for i in range(count) for j in range(i + 1)]
 
 
-def pack_half(out_ref, work):
-    blocks = lower_blocks(work.shape[0])
-    half = len(blocks) // 2
-    first = lax.axis_index("blk") == 0
-    for n in range(half):
-        (i, j), (k, l) = blocks[n], blocks[half + n]
-        mine = work[i * BASE : (i + 1) * BASE, j * BASE : (j + 1) * BASE]
-        other = work[k * BASE : (k + 1) * BASE, l * BASE : (l + 1) * BASE]
-        out_ref[n * BASE : (n + 1) * BASE, :] = jnp.where(first, mine, other)
+def pack(out_ref, work):
+    for n, (i, j) in enumerate(lower_blocks(work.shape[0])):
+        out_ref[n * BASE : (n + 1) * BASE, :] = work[i * BASE : (i + 1) * BASE, j * BASE : (j + 1) * BASE]
 
 
 def invert_pair_kernel(a_ref, b_ref, total_ref, out_ref, work, base):
     total_ref[...] = a_ref[...] + b_ref[...]
     work[...] = total_ref[...]
     sweep_all(work, base)
-    pack_half(out_ref, work)
+    pack(out_ref, work)
 
 
 def invert_kernel(a_ref, out_ref, work, base):
     work[...] = a_ref[...]
     sweep_all(work, base)
-    pack_half(out_ref, work)
+    pack(out_ref, work)
 
 
 def gate_kernel(*refs):
@@ -171,10 +165,10 @@
 def invert(ins, order):
     scratch = [pltpu.VMEM((order, order), jnp.float32), pltpu.VMEM((BASE, BASE), jnp.float32)]
     square = (order, order)
-    packed = (len(lower_blocks(order)) // 2 * BASE, BASE)
+    packed = (len(lower_blocks(order)) * BASE, BASE)
     if len(ins) == 2:
-        return local_call(invert_pair_kernel, ins, [square, packed], scratch, 40 * 10**9, "sum_invert", 20)
-    return [ins[0], local_call(invert_kernel, ins, [packed], scratch, 40 * 10**9, "invert", 20)[0]]
+        return local_call(invert_pair_kernel, ins, [square, packed], scratch, 40 * 10**9, "sum_invert", 12)
+    return [ins[0], local_call(invert_kernel, ins, [packed], scratch, 40 * 10**9, "invert", 12)[0]]
 
 
 def join(target, mine, other, index):
@@ -183,23 +177,21 @@
         target[:, pl.ds(pl.multiple_of(at * half, half), half)] = value[...]
 
 
-def unpack(target, mine, other, index):
-    blocks = lower_blocks(target.shape[0])
-    half = len(blocks) // 2
-    for n, (i, j) in enumerate(blocks):
-        place = slice(n % half * BASE, (n % half + 1) * BASE)
-        block = jnp.where(index == n // half, mine[place, :], other[place, :])
+def unpack(target, first, mine, other):
+    for n, (i, j) in enumerate(lower_blocks(target.shape[0])):
+        place = slice(n * BASE, (n + 1) * BASE)
+        block = jnp.where(first, mine[place, :], other[place, :])
         target[i * BASE : (i + 1) * BASE, j * BASE : (j + 1) * BASE] = block
         if i != j:
             target[j * BASE : (j + 1) * BASE, i * BASE : (i + 1) * BASE] = block.T
 
 
-def update_kernel(last, diag, low_a, low_b, high_a, high_b, both, link_b, both_low, both_high, next_b, new_diag, *rest):
+def update_kernel(last, diag, mine_in, other_in, both, link_b, both_low, both_high, next_b, new_diag, *rest):
     *new_both, low, high, link, nxt = rest
     index = lax.axis_index("blk")
     half = link_b.shape[1]
-    unpack(low, low_a, low_b, index)
-    unpack(high, high_a, high_b, index)
+    unpack(low, index == 0, mine_in, other_in)
+    unpack(high, index == 1, mine_in, other_in)
     join(link, both[:, :half], link_b, index)
     join(nxt, both_high[:, :half], next_b, index)
     mine = pl.ds(pl.multiple_of(index * half, half), half)
@@ -230,6 +222,15 @@
     return lax.ppermute(block, axis, route)
 
 
+def spread_both_ways(block, distance):
+    count = lax.axis_size("hor")
+    route = []
+    for i in range(count):
+        if i + distance < count:
+            route += [(2 * i, 2 * (i + distance)), (2 * (i + distance) + 1, 2 * i + 1)]
+    return lax.ppermute(block, ("hor", "blk"), route)
+
+
 def swapped(block):
     return lax.ppermute(block, "blk", [(0, 1), (1, 0)])
 
@@ -248,18 +249,16 @@
         distance = 2**depth
         both_low = shifted(both, "hor", distance)
         both_high = shifted(both, "hor", -distance)
+        link_other = swapped(both[:, :half])
         diag, mine = invert(ins, order)
-        mine = gated(mine, [both_low, both_high])
-        link_other = swapped(both[:, :half])
+        mine = gated(mine, [both_low, both_high, link_other])
         next_other = swapped(both_high[:, :half])
-        low = shifted(mine, "hor", distance)
-        high = shifted(mine, "hor", -distance)
-        low_other = swapped(low)
-        high_other = swapped(high)
+        mine = spread_both_ways(mine, distance)
+        other = swapped(mine)
         square = pltpu.VMEM((order, order), jnp.float32)
-        args = [diag, low, low_other, high, high_other, both, link_other, both_low, both_high, next_other]
+        args = [diag, mine, other, both, link_other, both_low, both_high, next_other]
         outs = [(order, half), (order, half), (order, width - half)] if last else [(order, order), (order, width)]
-        diag, *rest = local_call(functools.partial(update_kernel, last), args, outs, [square] * 4, 3 * 10**9, "update", 32)
+        diag, *rest = local_call(functools.partial(update_kernel, last), args, outs, [square] * 4, 3 * 10**9, "update", 28)
         ins, both = [diag], rest[0]
     return (diag[None], rest[0][None], rest[1][None])
 

time: 124 us -> 132 us (1.065)
  local copies, waits for them, and re-layouts: 9.56 us -> 15.3 us
  starting transfers between devices: 27.6 us -> 23.2 us
  waiting for transfers between devices: 32.9 us -> 37.1 us
    ppermute x0 -> x2, waiting for transfers between devices: none -> 23.7 us  [spread_both_ways(): return lax.ppermute(block, ('hor', 'blk'), route)]
    ppermute x8 -> x4, waiting for transfers between devices: 29.7 us -> 10.2 us  [shifted(): return lax.ppermute(block, axis, route)]
    ppermute x8 -> x4, starting transfers between devices: 25.8 us -> 13.2 us  [shifted(): return lax.ppermute(block, axis, route)]
    ppermute x0 -> x2, starting transfers between devices: none -> 8.12 us  [spread_both_ways(): return lax.ppermute(block, ('hor', 'blk'), route)]
    unnamed x32 -> x40, local copies, waits for them, and re-layouts: 8.41 us -> 13.1 us
    ppermute x9 -> x7, waiting for transfers between devices: 3.22 us -> 3.14 us  [swapped(): return lax.ppermute(block, 'blk', [(0, 1), (1, 0)])]
  transfers between devices with their start and end apart: 17 -> 13, of which waited for: 8 -> 5; matrix products, arithmetic and copies ran while one was open for 1% -> 2% of each run, Pallas kernels for 32% -> 31%
where the time goes in v4:
time: 132 us; the launch traced here: 130 us
  Pallas kernels  53.6 us (41%)
  waiting for transfers between devices  37.1 us (28%)
  starting transfers between devices  23.2 us (18%)
  local copies, waits for them, and re-layouts  15.3 us (12%)
    pallas_call x4, Pallas kernels, local_call(): pl.pallas_call(kernel, out_shape=[jax.ShapeDtypeStruct(s, jnp.float32) fo...  53.6 us
    ppermute x2, waiting for transfers between devices, spread_both_ways(): return lax.ppermute(block, ('hor', 'blk'), route)  23.7 us
    ppermute x4, starting transfers between devices, shifted(): return lax.ppermute(block, axis, route)  13.2 us
    unnamed x40, local copies, waits for them, and re-layouts  13.1 us
    ppermute x4, waiting for transfers between devices, shifted(): return lax.ppermute(block, axis, route)  10.2 us
    ppermute x2, starting transfers between devices, spread_both_ways(): return lax.ppermute(block, ('hor', 'blk'), route)  8.12 us
    ppermute x7, waiting for transfers between devices, swapped(): return lax.ppermute(block, 'blk', [(0, 1), (1, 0)])  3.14 us
  transfers between devices with their start and end apart: 13, of which 5 were waited for; matrix products, arithmetic and copies ran while one was open for 2% of the time, Pallas kernels for 31%

profile of v4, /device:TPU:0, one launch (start us, length us, event | category | flops | bytes accessed | tf_op | source)
XLA Modules:
  0.0 130.1 jit_solution(14391823960343803324)
XLA Ops:
  0.6 0.5 collective-permute-start
  1.3 0.8 copy-done.19
  2.2 1.3 collective-permute-start.2
  3.5 5.8 %collective-permute-start.1 = (f32[512,384]{1,0:T(8,128)S(1)}, f32[512,384]{1,0:T(8,128)S(1)}, u32[]{:S(2)}, u32[]{:S(2)}) collective-permute-start(f32[512,384]{1,0:T(8,128)S(1)} %pad_maximum_fusion.both), channel_id=1, source_target_pairs={{0,2},{2,4},{4,6},{6,8},{8,10},{10,12},{12,14},{1,3},{3,5},{5,7},{... | collective-permute-start | bytes 2359304 | tf_op jit(solution)/shard_map/ppermute | solution.py:222
  9.3 20.8 %sum_invert.1 = (f32[512,512]{1,0:T(8,128)S(1)}, f32[1280,128]{1,0:T(8,128)S(1)}) custom-call(f32[512,512]{1,0:T(8,128)S(1)} %bitcast.8, f32[512,512]{1,0:T(8,128)} %collective-permute-done.b_ref), custom_call_target="tpu_custom_call" | custom-call | flops 40000000000 | bytes 4194304 | tf_op jit(solution)/shard_map/sum_invert/pallas_call | solution.py:153
  30.1 0.9 copy-done.8
  31.0 1.0 copy-done.17
  32.0 10.2 %collective-permute-done.1.refs_1_.both_low = f32[512,384]{1,0:T(8,128)S(1)} collective-permute-done((f32[512,384]{1,0:T(8,128)S(1)}, f32[512,384]{1,0:T(8,128)S(1)}, u32[]{:S(2)}, u32[]{:S(2)}) %collective-permute-start.1) | collective-permute-done | bytes 786464 | tf_op jit(solution)/shard_map/ppermute | solution.py:222
  42.2 0.9 copy-done.4
  43.1 4.5 %collective-permute-start.4 = (f32[1280,128]{1,0:T(8,128)}, f32[1280,128]{1,0:T(8,128)S(1)}, u32[]{:S(2)}, u32[]{:S(2)}) collective-permute-start(f32[1280,128]{1,0:T(8,128)} %gate.2), channel_id=1, source_target_pairs={{0,2},{3,1},{2,4},{5,3},{4,6},{7,5},{6,8},{9,7},{8,10},{11,9},{10,... | collective-permute-start | bytes 1966088 | tf_op jit(solution)/shard_map/ppermute | solution.py:231
  47.6 15.3 %collective-permute-done.4.mine_in = f32[1280,128]{1,0:T(8,128)S(1)} collective-permute-done((f32[1280,128]{1,0:T(8,128)}, f32[1280,128]{1,0:T(8,128)S(1)}, u32[]{:S(2)}, u32[]{:S(2)}) %collective-permute-start.4) | collective-permute-done | bytes 655392 | tf_op jit(solution)/shard_map/ppermute | solution.py:231
  63.0 1.1 slice.12
  64.1 0.6 collective-permute-start.6
  64.7 1.5 %collective-permute-done.6.next_b = f32[512,256]{1,0:T(8,128)S(1)} collective-permute-done((f32[512,256]{1,0:T(8,128)S(1)}, f32[512,256]{1,0:T(8,128)S(1)}, u32[]{:S(2)}, u32[]{:S(2)}) %collective-permute-start.6) | collective-permute-done | bytes 524320 | tf_op jit(solution)/shard_map/ppermute | solution.py:235
  66.2 1.1 copy-done.5
  67.3 1.0 copy-done.11
  68.4 1.2 copy-done.18
  69.6 7.2 %update.2 = (f32[512,512]{1,0:T(8,128)S(1)}, f32[512,384]{1,0:T(8,128)S(1)}) custom-call(f32[512,512]{1,0:T(8,128)S(1)} %copy-done.18, f32[1280,128]{1,0:T(8,128)S(1)} %collective-permute-done.4.mine_in, f32[1280,128]{1,0:T(8,128)S(1)} %collective-permute-done.5.other_in, f32[512,384]{1,0:T(8,128)S(1)} %pad_maximum_fusion.both, f32[512,256]{1,0:T(8,128)S(1)} %copy-done.11, ...), custom_call_target="tpu_custom_call" | custom-call | flops 3000000000 | bytes 4194304 | tf_op jit(solution)/shard_map/update/pallas_call | solution.py:153
  76.9 1.3 collective-permute-start.8
  78.2 4.8 %collective-permute-start.7 = (f32[512,384]{1,0:T(8,128)S(1)}, f32[512,384]{1,0:T(8,128)S(1)}, u32[]{:S(2)}, u32[]{:S(2)}) collective-permute-start(f32[512,384]{1,0:T(8,128)S(1)} %get-tuple-element.13.both), channel_id=1, source_target_pairs={{0,4},{2,6},{4,8},{6,10},{8,12},{10,14},{1,5},{3,7},{5,9},{7,11},{... | collective-permute-start | bytes 2359304 | tf_op jit(solution)/shard_map/ppermute | solution.py:222
  83.1 19.5 %invert.1.refs_0_ = f32[1280,128]{1,0:T(8,128)S(1)} custom-call(f32[512,512]{1,0:T(8,128)S(1)} %get-tuple-element.12.a_ref.diag), custom_call_target="tpu_custom_call" | custom-call | flops 40000000000 | bytes 4194304 | tf_op jit(solution)/shard_map/invert/pallas_call | solution.py:153
  102.6 0.9 copy-done.9
  103.5 0.8 copy-done.12
  104.5 0.9 copy-done.6
  105.4 3.6 %collective-permute-start.10 = (f32[1280,128]{1,0:T(8,128)}, f32[1280,128]{1,0:T(8,128)S(1)}, u32[]{:S(2)}, u32[]{:S(2)}) collective-permute-start(f32[1280,128]{1,0:T(8,128)} %gate.3), channel_id=1, source_target_pairs={{0,4},{5,1},{2,6},{7,3},{4,8},{9,5},{6,10},{11,7},{8,12},{13,9},{1... | collective-permute-start | bytes 1966088 | tf_op jit(solution)/shard_map/ppermute | solution.py:231
  109.0 8.4 %collective-permute-done.10.mine_in = f32[1280,128]{1,0:T(8,128)S(1)} collective-permute-done((f32[1280,128]{1,0:T(8,128)}, f32[1280,128]{1,0:T(8,128)S(1)}, u32[]{:S(2)}, u32[]{:S(2)}) %collective-permute-start.10) | collective-permute-done | bytes 655392 | tf_op jit(solution)/shard_map/ppermute | solution.py:231
  117.6 1.1 slice.13
  119.0 1.6 %collective-permute-done.12.next_b = f32[512,256]{1,0:T(8,128)S(1)} collective-permute-done((f32[512,256]{1,0:T(8,128)S(1)}, f32[512,256]{1,0:T(8,128)S(1)}, u32[]{:S(2)}, u32[]{:S(2)}) %collective-permute-start.12) | collective-permute-done | bytes 524320 | tf_op jit(solution)/shard_map/ppermute | solution.py:235
  120.6 1.1 copy-done.7
  121.8 1.0 copy-done.13
  122.8 1.2 copy-done.16
  124.0 6.1 %update.3 = (f32[512,256]{1,0:T(8,128)}, f32[512,256]{1,0:T(8,128)}, f32[512,128]{1,0:T(8,128)}) custom-call(f32[512,512]{1,0:T(8,128)S(1)} %copy-done.16, f32[1280,128]{1,0:T(8,128)S(1)} %collective-permute-done.10.mine_in, f32[1280,128]{1,0:T(8,128)S(1)} %collective-permute-done.11.other_in, f32[512,384]{1,0:T(8,128)S(1)} %get-tuple-element.13.both, ...), custom_call_target="tpu_custom_call" | custom-call | flops 3000000000 | bytes 4194304 | tf_op jit(solution)/shard_map/update/pallas_call | solution.py:153
  (45 shorter events, 1.2 us)
Async XLA Ops:
  0.6 8.7 %collective-permute-start = (f32[512,512]{1,0:T(8,128)}, f32[512,512]{1,0:T(8,128)}, u32[]{:S(2)}, u32[]{:S(2)}) collective-permute-start(f32[512,512]{1,0:T(8,128)} %bitcast.7), channel_id=1, source_target_pairs={{0,1},{1,0},{2,3},{3,2},{4,5},{5,4},{6,7},{7,6},{8,9},{9,8},{10,11... | collective-permute-start | bytes 3145736 | tf_op jit(solution)/shard_map/ppermute | solution.py:235
  1.1 0.9 copy-start.19
  1.2 8.1 %copy-start.14 = (f32[1,512,512]{2,1,0:T(8,128)S(1)}, f32[1,512,512]{2,1,0:T(8,128)}, u32[]{:S(2)}) copy-start(f32[1,512,512]{2,1,0:T(8,128)} %param.3) | copy-start | bytes 3145732
  1.2 30.8 %collective-permute-start.3 = (f32[512,256]{1,0:T(8,128)S(1)}, f32[512,256]{1,0:T(8,128)S(1)}, u32[]{:S(2)}, u32[]{:S(2)}) collective-permute-start(f32[512,256]{1,0:T(8,128)S(1)} %select_bitcast_fusion), channel_id=1, source_target_pairs={{0,1},{1,0},{2,3},{3,2},{4,5},{5,4},{6,7},{7,6},{8,9},{9,8},{10,11... | collective-permute-start | bytes 1572872 | tf_op jit(solution)/shard_map/ppermute | solution.py:235
  2.2 29.8 %collective-permute-start.2 = (f32[512,384]{1,0:T(8,128)S(1)}, f32[512,384]{1,0:T(8,128)S(1)}, u32[]{:S(2)}, u32[]{:S(2)}) collective-permute-start(f32[512,384]{1,0:T(8,128)S(1)} %pad_maximum_fusion.both), channel_id=1, source_target_pairs={{2,0},{4,2},{6,4},{8,6},{10,8},{12,10},{14,12},{3,1},{5,3},{7,5},{... | collective-permute-start | bytes 2359304 | tf_op jit(solution)/shard_map/ppermute | solution.py:222
  3.5 38.7 %collective-permute-start.1 = (f32[512,384]{1,0:T(8,128)S(1)}, f32[512,384]{1,0:T(8,128)S(1)}, u32[]{:S(2)}, u32[]{:S(2)}) collective-permute-start(f32[512,384]{1,0:T(8,128)S(1)} %pad_maximum_fusion.both), channel_id=1, source_target_pairs={{0,2},{2,4},{4,6},{6,8},{8,10},{10,12},{12,14},{1,3},{3,5},{5,7},{... | collective-permute-start | bytes 2359304 | tf_op jit(solution)/shard_map/ppermute | solution.py:222
  30.1 0.9 copy-start.8
  31.0 1.0 copy-start.17
  32.0 10.2 %copy-start.10 = (f32[512,256]{1,0:T(8,128)}, f32[512,256]{1,0:T(8,128)S(1)}, u32[]{:S(2)}) copy-start(f32[512,256]{1,0:T(8,128)S(1)} %collective-permute-done.3.refs_3_.link_b) | copy-start | bytes 1572868
  32.0 10.2 %copy-start = (f32[512,384]{1,0:T(8,128)}, f32[512,384]{1,0:T(8,128)S(1)}, u32[]{:S(2)}) copy-start(f32[512,384]{1,0:T(8,128)S(1)} %collective-permute-done.2.refs_2_.both_high) | copy-start | bytes 2359300
  42.2 0.9 copy-start.4
  43.1 23.1 %copy-start.1 = (f32[512,384]{1,0:T(8,128)S(1)}, f32[512,384]{1,0:T(8,128)}, u32[]{:S(2)}) copy-start(f32[512,384]{1,0:T(8,128)} %copy-done) | copy-start | bytes 2359300
  43.1 19.9 %collective-permute-start.4 = (f32[1280,128]{1,0:T(8,128)}, f32[1280,128]{1,0:T(8,128)S(1)}, u32[]{:S(2)}, u32[]{:S(2)}) collective-permute-start(f32[1280,128]{1,0:T(8,128)} %gate.2), channel_id=1, source_target_pairs={{0,2},{3,1},{2,4},{5,3},{4,6},{7,5},{6,8},{9,7},{8,10},{11,9},{10,... | collective-permute-start | bytes 1966088 | tf_op jit(solution)/shard_map/ppermute | solution.py:231
  63.0 3.2 %collective-permute-start.5 = (f32[1280,128]{1,0:T(8,128)S(1)}, f32[1280,128]{1,0:T(8,128)S(1)}, u32[]{:S(2)}, u32[]{:S(2)}) collective-permute-start(f32[1280,128]{1,0:T(8,128)S(1)} %collective-permute-done.4.mine_in), channel_id=1, source_target_pairs={{0,1},{1,0},{2,3},{3,2},{4,5},{5,4},{6,7},{7,6},{8,9},{9,8},{10,11... | collective-permute-start | bytes 1966088 | tf_op jit(solution)/shard_map/ppermute | solution.py:235
  64.1 2.1 %collective-permute-start.6 = (f32[512,256]{1,0:T(8,128)S(1)}, f32[512,256]{1,0:T(8,128)S(1)}, u32[]{:S(2)}, u32[]{:S(2)}) collective-permute-start(f32[512,256]{1,0:T(8,128)S(1)} %slice.12), channel_id=1, source_target_pairs={{0,1},{1,0},{2,3},{3,2},{4,5},{5,4},{6,7},{7,6},{8,9},{9,8},{10,11... | collective-permute-start | bytes 1572872 | tf_op jit(solution)/shard_map/ppermute | solution.py:235
  66.2 1.1 copy-start.5
  67.3 1.0 copy-start.11
  68.4 1.2 copy-start.18
  76.8 25.7 %copy-start.15 = (f32[512,512]{1,0:T(8,128)}, f32[512,512]{1,0:T(8,128)S(1)}, u32[]{:S(2)}) copy-start(f32[512,512]{1,0:T(8,128)S(1)} %get-tuple-element.12.a_ref.diag) | copy-start | bytes 3145732
  76.9 26.6 %collective-permute-start.8 = (f32[512,384]{1,0:T(8,128)S(1)}, f32[512,384]{1,0:T(8,128)S(1)}, u32[]{:S(2)}, u32[]{:S(2)}) collective-permute-start(f32[512,384]{1,0:T(8,128)S(1)} %get-tuple-element.13.both), channel_id=1, source_target_pairs={{4,0},{6,2},{8,4},{10,6},{12,8},{14,10},{5,1},{7,3},{9,5},{11,7},{... | collective-permute-start | bytes 2359304 | tf_op jit(solution)/shard_map/ppermute | solution.py:222
  78.2 25.3 %collective-permute-start.7 = (f32[512,384]{1,0:T(8,128)S(1)}, f32[512,384]{1,0:T(8,128)S(1)}, u32[]{:S(2)}, u32[]{:S(2)}) collective-permute-start(f32[512,384]{1,0:T(8,128)S(1)} %get-tuple-element.13.both), channel_id=1, source_target_pairs={{0,4},{2,6},{4,8},{6,10},{8,12},{10,14},{1,5},{3,7},{5,9},{7,11},{... | collective-permute-start | bytes 2359304 | tf_op jit(solution)/shard_map/ppermute | solution.py:222
  83.0 20.5 %collective-permute-start.9 = (f32[512,256]{1,0:T(8,128)S(1)}, f32[512,256]{1,0:T(8,128)S(1)}, u32[]{:S(2)}, u32[]{:S(2)}) collective-permute-start(f32[512,256]{1,0:T(8,128)S(1)} %slice.10), channel_id=1, source_target_pairs={{0,1},{1,0},{2,3},{3,2},{4,5},{5,4},{6,7},{7,6},{8,9},{9,8},{10,11... | collective-permute-start | bytes 1572872 | tf_op jit(solution)/shard_map/ppermute | solution.py:235
  102.6 0.9 copy-start.9
  103.4 1.1 copy-start.2
  104.5 0.9 copy-start.6
  105.4 15.2 %copy-start.3 = (f32[512,384]{1,0:T(8,128)S(1)}, f32[512,384]{1,0:T(8,128)}, u32[]{:S(2)}) copy-start(f32[512,384]{1,0:T(8,128)} %copy-done.2) | copy-start | bytes 2359300
  105.4 12.0 %collective-permute-start.10 = (f32[1280,128]{1,0:T(8,128)}, f32[1280,128]{1,0:T(8,128)S(1)}, u32[]{:S(2)}, u32[]{:S(2)}) collective-permute-start(f32[1280,128]{1,0:T(8,128)} %gate.3), channel_id=1, source_target_pairs={{0,4},{5,1},{2,6},{7,3},{4,8},{9,5},{6,10},{11,7},{8,12},{13,9},{1... | collective-permute-start | bytes 1966088 | tf_op jit(solution)/shard_map/ppermute | solution.py:231
  117.4 3.3 %collective-permute-start.11 = (f32[1280,128]{1,0:T(8,128)S(1)}, f32[1280,128]{1,0:T(8,128)S(1)}, u32[]{:S(2)}, u32[]{:S(2)}) collective-permute-start(f32[1280,128]{1,0:T(8,128)S(1)} %collective-permute-done.10.mine_in), channel_id=1, source_target_pairs={{0,1},{1,0},{2,3},{3,2},{4,5},{5,4},{6,7},{7,6},{8,9},{9,8},{10,11... | collective-permute-start | bytes 1966088 | tf_op jit(solution)/shard_map/ppermute | solution.py:235
  118.6 2.0 %collective-permute-start.12 = (f32[512,256]{1,0:T(8,128)S(1)}, f32[512,256]{1,0:T(8,128)S(1)}, u32[]{:S(2)}, u32[]{:S(2)}) collective-permute-start(f32[512,256]{1,0:T(8,128)S(1)} %slice.13), channel_id=1, source_target_pairs={{0,1},{1,0},{2,3},{3,2},{4,5},{5,4},{6,7},{7,6},{8,9},{9,8},{10,11... | collective-permute-start | bytes 1572872 | tf_op jit(solution)/shard_map/ppermute | solution.py:235
  120.6 1.1 copy-start.7
  121.8 1.0 copy-start.13
  122.8 1.2 copy-start.16
  (1 other events, 0.8 us)
